TPU v7x, 128 devices: a whole 4x4x4 slice. The times are simulated.
128 devices in a mesh: dom: 128 (over y, z, x, core).
Axes of the slice: x: 4, y: 4, z: 4, core: 2. Of those that a mesh axis runs over, the one named last changes fastest.
Arguments:
- dofs: float32 [9, 35, 49152], P(None, None, 'dom'), may hold values from -6 to 6
- star: float32 [3, 9, 9, 49152], P(None, None, None, 'dom'), may hold values from -0.6 to 0.6
- flux_minus: float32 [4, 9, 9, 49152], P(None, None, None, 'dom'), may hold values from -0.6 to 0.6
- flux_plus: float32 [4, 9, 9, 49152], P(None, None, None, 'dom'), may hold values from -0.6 to 0.6
- cluster: int32 [49152], P('dom'), may hold values from 0 to 2, as said below
- neighbour: int32 [4, 49152], P(None, 'dom'), may hold values from 0 to 639, as said below
- face_code: int32 [4, 49152], P(None, 'dom'), may hold values from 0 to 11
- send_list: int32 [8, 4096], P(None, 'dom'), may hold values from 0 to 383
- stiffness: float32 [3, 35, 35], replicated, may hold values from -1 to 1
- face_proj: float32 [4, 15, 35], replicated, may hold values from -1 to 1
- face_lift: float32 [4, 35, 15], replicated, may hold values from -1.5 to 1.5
- face_turn: float32 [3, 15, 15], replicated, may hold values from -1.5 to 1.5
Outputs:
- new_dofs: float32 [9, 35, 49152], P(None, None, 'dom')
Inputs may be any that keep to these rules, and one draw needn't show every extreme that they name: `cluster`: every partition holds at most 128 fast elements, and one partition holds exactly 128. `neighbour`: A ghost slot never names a partition outside 0 .. 128 - 1.
All inputs are finite; a program needn't handle non-finite values.
Results may differ from a plain program's by a relative error of at most 0.0003.
Values sent between devices are 32-bit elements; how exact they have to be, the bound alone decides.
No kernel may reach another device: no remote copies, remote signals or barrier semaphores. Data moves between devices by JAX's collectives and lax.ppermute only.
A program may use at most 256 MiB of HBM per device.

v0:
```python
import math

import jax
import jax.numpy as jnp
from jax import lax
from jax.sharding import PartitionSpec as P

ORDER = 5
RADIUS = 4


HIGH = lax.Precision.HIGHEST


def passed_along(value, axis, steps):
    count = lax.axis_size(axis)
    first, last = (max(0, -steps), min(count, count - steps))
    return lax.ppermute(value, axis, [(source, source + steps) for source in range(first, last)])


def derivatives(field, star, stiffness):
    terms = [field]
    current = field
    for level in range(ORDER - 1):
        spread = jnp.einsum("dbc,qce->dqbe", stiffness, current, precision=HIGH)
        current = -jnp.einsum("dpqe,dqbe->pbe", star, spread, precision=HIGH)
        terms.append(current)
    return terms


def integral(terms, start, finish):
    total = terms[0] * (finish - start)
    for level in range(1, len(terms)):
        factor = (finish ** (level + 1) - start ** (level + 1)) / math.factorial(level + 1)
        total = total + terms[level] * factor
    return total


def update(field, own, nearby, elements, tables):
    star, minus, plus, codes = elements
    stiffness, face_proj, face_lift, face_turn = tables
    spread = jnp.einsum("dcb,qce->dqbe", stiffness, own, precision=HIGH)
    volume = jnp.einsum("dpqe,dqbe->pbe", star, spread, precision=HIGH)
    local = jnp.einsum("igc,qce->iqge", face_proj, own, precision=HIGH)
    local = jnp.einsum("ipqe,iqge->ipge", minus, local, precision=HIGH)
    local = jnp.einsum("ibg,ipge->pbe", face_lift, local, precision=HIGH)
    every = jnp.einsum("jgc,iqce->ijqge", face_proj, nearby, precision=HIGH)
    pick_face = (codes[:, None, :] // 3 == jnp.arange(4, dtype=jnp.int32)[None, :, None]).astype(
        field.dtype
    )
    chosen = jnp.einsum("ije,ijqge->iqge", pick_face, every, precision=HIGH)
    turned = jnp.einsum("hgk,iqke->ihqge", face_turn, chosen, precision=HIGH)
    pick_turn = (codes[:, None, :] % 3 == jnp.arange(3, dtype=jnp.int32)[None, :, None]).astype(
        field.dtype
    )
    chosen = jnp.einsum("ihe,ihqge->iqge", pick_turn, turned, precision=HIGH)
    remote = jnp.einsum("ipqe,iqge->ipge", plus, chosen, precision=HIGH)
    remote = jnp.einsum("ibg,ipge->pbe", face_lift, remote, precision=HIGH)
    return field + volume - local - remote


def ghosts(field, send_list):
    outgoing = jnp.moveaxis(jnp.take(field, send_list, axis=2), 2, 0)
    offsets = list(range(-RADIUS, 0)) + list(range(1, RADIUS + 1))
    received = [
        passed_along(outgoing[place], "dom", offset) for place, offset in enumerate(offsets)
    ]
    stacked = jnp.stack(received, axis=2)
    return jnp.concatenate([field, stacked.reshape(field.shape[0], field.shape[1], -1)], axis=2)


def beside_all(extended, rows):
    return jnp.moveaxis(jnp.take(extended, rows, axis=2), 2, 0)


def body(
    dofs,
    star,
    flux_minus,
    flux_plus,
    cluster,
    neighbour,
    face_code,
    send_list,
    stiffness,
    face_proj,
    face_lift,
    face_turn,
):
    tables = (stiffness, face_proj, face_lift, face_turn)
    every_element = (star, flux_minus, flux_plus, face_code)
    terms = derivatives(dofs, star, stiffness)
    early = integral(terms, 0.0, 1.0)
    later = integral(terms, 1.0, 2.0)
    reach_early = ghosts(early, send_list)
    fast = cluster == 0
    medium = cluster == 1
    near_early = beside_all(reach_early, neighbour)
    moved = jnp.where(fast, update(dofs, early, near_early, every_element, tables), dofs)
    late = jnp.where(fast, integral(derivatives(moved, star, stiffness), 0.0, 1.0), later)
    reach_late = ghosts(late, send_list)
    near_late = beside_all(reach_late, neighbour)
    start_field = jnp.where(fast, moved, dofs)
    own_integral = jnp.where(fast, late, early + late)
    near_integral = jnp.where(fast[None, None, None, :], near_late, near_early + near_late)
    stepped = update(start_field, own_integral, near_integral, every_element, tables)
    result = jnp.where(fast | medium, stepped, dofs)
    return result


def solution(mesh):
    return jax.shard_map(
        body,
        mesh=mesh,
        in_specs=(
            P(None, None, "dom"),
            P(None, None, None, "dom"),
            P(None, None, None, "dom"),
            P(None, None, None, "dom"),
            P("dom"),
            P(None, "dom"),
            P(None, "dom"),
            P(None, "dom"),
            P(),
            P(),
            P(),
            P(),
        ),
        out_specs=P(None, None, "dom"),
        check_vma=False,
    )
```

profile of v0, /device:TPU:25, one launch (start us, length us, event | category | flops | bytes accessed | tf_op | source)
XLA Modules:
  0.0 683.4 jit_solution(8975396789528935419)
XLA Ops:
  1.4 6.8 copy.236
  15.5 7.3 %copy.235 = f32[3,9,35,384]{2,1,0,3:T(8,128)} copy(f32[3,9,35,384]{3,2,0,1:T(8,128)} %convolution_bitcast_fusion.4) | data formatting | bytes 2903040 | tf_op jit(solution)/shard_map/dbc,qce->dqbe/transpose | solution.py:25
  22.7 14.7 %fusion.130 = f32[384,35,9,1]{1,2,3,0:T(8,128)S(1)} fusion(f32[3,9,35,384]{2,1,0,3:T(8,128)} %copy.235, f32[3,9,9,384]{2,1,0,3:T(8,128)} %copy.236), kind=kOutput, calls=%fused_computation.200 | convolution fusion | flops 39191040 | bytes 2308608 | tf_op jit(solution)/shard_map/dpqe,dqbe->pbe/dot_general | solution.py:26
  42.6 7.3 %copy.239 = f32[3,9,35,384]{2,1,0,3:T(8,128)} copy(f32[3,9,35,384]{3,2,0,1:T(8,128)} %fusion.62) | data formatting | bytes 2903040 | tf_op jit(solution)/shard_map/dbc,qce->dqbe/transpose | solution.py:25
  49.9 14.8 %fusion.131 = f32[384,35,9,1]{1,2,3,0:T(8,128)S(1)} fusion(f32[3,9,35,384]{2,1,0,3:T(8,128)} %copy.239, f32[3,9,9,384]{2,1,0,3:T(8,128)} %copy.236), kind=kOutput, calls=%fused_computation.201 | convolution fusion | flops 39191040 | bytes 2308608 | tf_op jit(solution)/shard_map/dpqe,dqbe->pbe/dot_general | solution.py:26
  69.9 7.3 %copy.242 = f32[3,9,35,384]{2,1,0,3:T(8,128)} copy(f32[3,9,35,384]{3,2,0,1:T(8,128)} %fusion.65) | data formatting | bytes 2903040 | tf_op jit(solution)/shard_map/dbc,qce->dqbe/transpose | solution.py:25
  77.2 15.0 %fusion.132 = f32[384,35,9,1]{1,2,3,0:T(8,128)S(1)} fusion(f32[3,9,35,384]{2,1,0,3:T(8,128)} %copy.242, f32[3,9,9,384]{2,1,0,3:T(8,128)} %copy.236), kind=kOutput, calls=%fused_computation.202 | convolution fusion | flops 39191040 | bytes 2308608 | tf_op jit(solution)/shard_map/dpqe,dqbe->pbe/dot_general | solution.py:26
  97.5 7.3 %copy.245 = f32[3,9,35,384]{2,1,0,3:T(8,128)} copy(f32[3,9,35,384]{3,2,0,1:T(8,128)} %fusion.68) | data formatting | bytes 2903040 | tf_op jit(solution)/shard_map/dbc,qce->dqbe/transpose | solution.py:25
  104.9 18.4 %bitcast_add_fusion.4 = (f32[9,35,384]{1,0,2:T(8,128)}, f32[384,35,9,1]{1,2,3,0:T(8,128)}) fusion(f32[9,35,384]{1,0,2:T(8,128)S(1)} %copy.251, f32[384,35,9,1]{1,2,3,0:T(8,128)} %copy-done.2, f32[384,35,9,1]{1,2,3,0:T(8,128)} %copy-done.3, f32[384,35,9,1]{1,2,3,0:T(8,128)} %copy-done.4, f32[3,9,35,384]{2,1,0,3:T(8,128)} %copy.245, f32[3,9,9,384]{2,1,0,3:T(8,128)} %copy.236), kind=kOutput, calls=%fused_computation.43 | convolution fusion | flops 40642560 | bytes 4727808 | tf_op jit(solution)/shard_map/dpqe,dqbe->pbe/dot_general | solution.py:26
  130.3 8.4 %collective-permute-start = (f32[9,35,32]{1,2,0:T(8,128)}, f32[9,35,32]{1,2,0:T(8,128)}, u32[]{:S(2)}, u32[]{:S(2)}) collective-permute-start(f32[9,35,32]{1,2,0:T(8,128)} %get-tuple-element.22), channel_id=1, source_target_pairs={{4,0},{5,1},{6,2},{7,3},{8,4},{9,5},{10,6},{11,7},{12,8},{13,9},{1... | collective-permute-start | bytes 120968 | tf_op jit(solution)/shard_map/ppermute | solution.py:18
  159.8 8.4 %copy.254 = f32[4,9,15,384]{1,2,3,0:T(8,128)} copy(f32[4,9,15,384]{3,2,0,1:T(8,128)} %convolution_bitcast_fusion.6) | data formatting | bytes 1658880 | tf_op jit(solution)/shard_map/igc,qce->iqge/transpose | solution.py:44
  168.2 7.9 %copy.255 = f32[4,9,9,384]{2,1,3,0:T(8,128)} copy(f32[4,9,9,384]{3,0,2,1:T(4,128)} %param.18) | data formatting | bytes 995328 | tf_op args[2]
  176.1 25.9 %convolution_bitcast_fusion.1 = f32[4,9,15,384]{1,2,3,0:T(8,128)} fusion(f32[4,9,15,384]{1,2,3,0:T(8,128)} %copy.254, f32[4,9,9,384]{2,1,3,0:T(8,128)} %copy.255), kind=kOutput, calls=%fused_computation.14 | convolution fusion | flops 22394880 | bytes 2156544 | tf_op jit(solution)/shard_map/ipqe,iqge->ipge/dot_general | solution.py:45
  202.0 9.4 %copy.256 = f32[4,9,15,384]{3,2,0,1:T(8,128)} copy(f32[4,9,15,384]{1,2,3,0:T(8,128)} %convolution_bitcast_fusion.1) | data formatting | bytes 1658880 | tf_op jit(solution)/shard_map/ipqe,iqge->ipge/transpose | solution.py:45
  214.7 7.8 %copy.270 = f32[4,9,9,384]{2,1,3,0:T(8,128)} copy(f32[4,9,9,384]{3,0,2,1:T(4,128)} %param.19) | data formatting | bytes 995328 | tf_op args[3]
  225.8 7.2 %copy.249 = f32[3,9,35,384]{2,1,0,3:T(8,128)} copy(f32[3,9,35,384]{3,2,0,1:T(8,128)} %convolution_bitcast_fusion.3) | data formatting | bytes 2903040 | tf_op jit(solution)/shard_map/dcb,qce->dqbe/transpose | solution.py:42
  241.6 4.0 collective-permute-start.7
  249.3 4.4 collective-permute-done.7
  257.1 11.1 %gather_fusion.1 = f32[1536,9,35]{2,1,0:T(8,128)} fusion(f32[9,35,640]{1,0,2:T(8,128)} %pad_maximum_fusion, s32[2048]{0:T(1024)S(1)} %pad_clamp_fusion), kind=kCustom, calls=%fused_computation.1.clone | custom fusion | bytes 3876864 | tf_op jit(solution)/shard_map/jit(_take)/gather | solution.py:73
  268.3 8.2 %copy.268 = f32[4,384,9,35]{1,3,2,0:T(8,128)} copy(f32[4,384,9,35]{3,2,1,0:T(8,128)} %bitcast.506) | data formatting | bytes 3870720 | tf_op jit(solution)/shard_map/jit(_take)/gather | solution.py:73
  276.5 4.8 fusion.11
  284.6 8.4 %copy.348 = f32[4,384,9,15]{2,3,1,0:T(8,128)} copy(f32[4,384,9,15]{1,3,2,0:T(8,128)} %fusion.37) | data formatting | bytes 1658880 | tf_op jit(solution)/shard_map/ihe,ihqge->iqge/dot_general | solution.py:56
  293.0 26.1 %fusion.4 = f32[4,9,15,384]{1,2,3,0:T(8,128)} fusion(f32[4,9,9,384]{2,1,3,0:T(8,128)} %copy.270, f32[4,384,9,15]{2,3,1,0:T(8,128)} %copy.348), kind=kOutput, calls=%fused_computation.11 | convolution fusion | flops 22394880 | bytes 2156544 | tf_op jit(solution)/shard_map/ipqe,iqge->ipge/dot_general | solution.py:57
  319.1 9.0 %copy.271 = f32[4,9,15,384]{3,2,0,1:T(8,128)} copy(f32[4,9,15,384]{1,2,3,0:T(8,128)} %fusion.4) | data formatting | bytes 1658880 | tf_op jit(solution)/shard_map/ipqe,iqge->ipge/transpose | solution.py:57
  334.0 16.5 %fusion.18 = f32[9,35,384]{1,0,2:T(8,128)S(1)} fusion(f32[9,35,384]{1,0,2:T(8,128)S(1)} %copy.251, f32[9,384,35]{2,0,1:T(8,128)} %copy.273, f32[9,384,35]{2,0,1:T(8,128)} %copy.258, f32[3,9,35,384]{2,1,0,3:T(8,128)} %copy.249, f32[3,9,9,384]{2,1,0,3:T(8,128)} %copy.236, pred[384]{0:T(512)(128)(4,1)S(1)} %get-tuple-element.26), kind=kOutput, calls=%fused_computation.28 | convolution fusion | flops 39674880 | bytes 3760512 | tf_op jit(solution)/shard_map/dpqe,dqbe->pbe/dot_general | solution.py:43
  355.7 7.2 %copy.277 = f32[3,9,35,384]{2,1,0,3:T(8,128)} copy(f32[3,9,35,384]{3,2,0,1:T(8,128)} %fusion.71) | data formatting | bytes 2903040 | tf_op jit(solution)/shard_map/dbc,qce->dqbe/transpose | solution.py:25
  362.9 14.9 %fusion.133 = f32[384,35,9,1]{1,2,3,0:T(8,128)S(1)} fusion(f32[3,9,35,384]{2,1,0,3:T(8,128)} %copy.277, f32[3,9,9,384]{2,1,0,3:T(8,128)} %copy.236), kind=kOutput, calls=%fused_computation.203 | convolution fusion | flops 39191040 | bytes 2308608 | tf_op jit(solution)/shard_map/dpqe,dqbe->pbe/dot_general | solution.py:26
  383.0 7.2 %copy.280 = f32[3,9,35,384]{2,1,0,3:T(8,128)} copy(f32[3,9,35,384]{3,2,0,1:T(8,128)} %fusion.74) | data formatting | bytes 2903040 | tf_op jit(solution)/shard_map/dbc,qce->dqbe/transpose | solution.py:25
  390.2 15.1 %fusion.134 = f32[384,35,9,1]{1,2,3,0:T(8,128)S(1)} fusion(f32[3,9,35,384]{2,1,0,3:T(8,128)} %copy.280, f32[3,9,9,384]{2,1,0,3:T(8,128)} %copy.236), kind=kOutput, calls=%fused_computation.204 | convolution fusion | flops 39191040 | bytes 2308608 | tf_op jit(solution)/shard_map/dpqe,dqbe->pbe/dot_general | solution.py:26
  410.5 7.2 %copy.283 = f32[3,9,35,384]{2,1,0,3:T(8,128)} copy(f32[3,9,35,384]{3,2,0,1:T(8,128)} %fusion.77) | data formatting | bytes 2903040 | tf_op jit(solution)/shard_map/dbc,qce->dqbe/transpose | solution.py:25
  417.8 14.8 %fusion.135 = f32[384,35,9,1]{1,2,3,0:T(8,128)S(1)} fusion(f32[3,9,35,384]{2,1,0,3:T(8,128)} %copy.283, f32[3,9,9,384]{2,1,0,3:T(8,128)} %copy.236), kind=kOutput, calls=%fused_computation.205 | convolution fusion | flops 39191040 | bytes 2308608 | tf_op jit(solution)/shard_map/dpqe,dqbe->pbe/dot_general | solution.py:26
  437.7 7.2 %copy.286 = f32[3,9,35,384]{2,1,0,3:T(8,128)} copy(f32[3,9,35,384]{3,2,0,1:T(8,128)} %fusion.80) | data formatting | bytes 2903040 | tf_op jit(solution)/shard_map/dbc,qce->dqbe/transpose | solution.py:25
  444.9 22.0 %fusion.19 = f32[9,35,384]{1,0,2:T(8,128)} fusion(f32[9,35,384]{1,0,2:T(8,128)} %copy-done.5, f32[9,35,384]{1,0,2:T(8,128)S(1)} %copy.251, f32[384,35,9,1]{1,2,3,0:T(8,128)} %get-tuple-element.28, f32[384,35,9,1]{1,2,3,0:T(8,128)} %copy-done.7, f32[384,35,9,1]{1,2,3,0:T(8,128)} %copy-done.8, f32[384,35,9,1]{1,2,3,0:T(8,128)} %copy-done.9, ...), kind=kOutput, calls=%fused_computation.30 | convolution fusion | flops 42215040 | bytes 6663552 | tf_op jit(solution)/shard_map/dpqe,dqbe->pbe/dot_general | solution.py:26
  466.9 4.7 fusion.12
  485.2 8.4 %copy.295 = f32[4,9,15,384]{1,2,3,0:T(8,128)} copy(f32[4,9,15,384]{3,2,0,1:T(8,128)} %convolution_bitcast_fusion.5) | data formatting | bytes 1658880 | tf_op jit(solution)/shard_map/igc,qce->iqge/transpose | solution.py:44
  493.6 26.3 %convolution_bitcast_fusion = f32[4,9,15,384]{1,2,3,0:T(8,128)} fusion(f32[4,9,15,384]{1,2,3,0:T(8,128)} %copy.295, f32[4,9,9,384]{2,1,3,0:T(8,128)} %copy.255), kind=kOutput, calls=%fused_computation.13 | convolution fusion | flops 22394880 | bytes 2156544 | tf_op jit(solution)/shard_map/ipqe,iqge->ipge/dot_general | solution.py:45
  520.0 9.0 %copy.297 = f32[4,9,15,384]{3,2,0,1:T(8,128)} copy(f32[4,9,15,384]{1,2,3,0:T(8,128)} %convolution_bitcast_fusion) | data formatting | bytes 1658880 | tf_op jit(solution)/shard_map/ipqe,iqge->ipge/transpose | solution.py:45
  539.2 7.2 %copy.291 = f32[3,9,35,384]{2,1,0,3:T(8,128)} copy(f32[3,9,35,384]{3,2,0,1:T(8,128)} %convolution_bitcast_fusion.2) | data formatting | bytes 2903040 | tf_op jit(solution)/shard_map/dcb,qce->dqbe/transpose | solution.py:42
  546.4 6.9 %collective-permute-start.9 = (f32[9,35,32]{1,2,0:T(8,128)}, f32[9,35,32]{1,2,0:T(8,128)S(1)}, u32[]{:S(2)}, u32[]{:S(2)}) collective-permute-start(f32[9,35,32]{1,2,0:T(8,128)} %get-tuple-element.13), channel_id=1, source_target_pairs={{3,0},{4,1},{5,2},{6,3},{7,4},{8,5},{9,6},{10,7},{11,8},{12,9},{13... | collective-permute-start | bytes 120968 | tf_op jit(solution)/shard_map/ppermute | solution.py:18
  567.4 4.5 collective-permute-start.15
  572.3 7.4 %collective-permute-done.14 = f32[9,35,32]{1,2,0:T(8,128)S(1)} collective-permute-done((f32[9,35,32]{1,2,0:T(8,128)}, f32[9,35,32]{1,2,0:T(8,128)S(1)}, u32[]{:S(2)}, u32[]{:S(2)}) %collective-permute-start.14) | collective-permute-done | bytes 40352 | tf_op jit(solution)/shard_map/ppermute | solution.py:18
  583.4 11.2 %gather_fusion.3 = f32[1536,9,35]{2,1,0:T(8,128)} fusion(f32[9,35,640]{1,0,2:T(8,128)} %pad_maximum_fusion.1, s32[2048]{0:T(1024)S(1)} %pad_clamp_fusion), kind=kCustom, calls=%fused_computation.3.clone | custom fusion | bytes 3876864 | tf_op jit(solution)/shard_map/jit(_take)/gather | solution.py:73
  594.6 8.3 %copy.309 = f32[4,384,9,35]{1,3,2,0:T(8,128)} copy(f32[4,384,9,35]{3,2,1,0:T(8,128)} %bitcast.505) | data formatting | bytes 3870720 | tf_op jit(solution)/shard_map/jit(_take)/gather | solution.py:73
  602.9 5.9 fusion.10
  612.1 8.4 %copy.380 = f32[4,384,9,15]{2,3,1,0:T(8,128)} copy(f32[4,384,9,15]{1,3,2,0:T(8,128)} %fusion.36) | data formatting | bytes 1658880 | tf_op jit(solution)/shard_map/ihe,ihqge->iqge/dot_general | solution.py:56
  620.5 26.1 %fusion.7 = f32[4,9,15,384]{1,2,3,0:T(8,128)} fusion(f32[4,9,9,384]{2,1,3,0:T(8,128)} %copy.270, f32[4,384,9,15]{2,3,1,0:T(8,128)} %copy.380), kind=kOutput, calls=%fused_computation.12 | convolution fusion | flops 22394880 | bytes 2156544 | tf_op jit(solution)/shard_map/ipqe,iqge->ipge/dot_general | solution.py:57
  646.6 9.0 %copy.312 = f32[4,9,15,384]{3,2,0,1:T(8,128)} copy(f32[4,9,15,384]{1,2,3,0:T(8,128)} %fusion.7) | data formatting | bytes 1658880 | tf_op jit(solution)/shard_map/ipqe,iqge->ipge/transpose | solution.py:57
  661.6 18.4 %fusion.15 = f32[9,35,384]{1,0,2:T(8,128)} fusion(f32[9,35,384]{1,0,2:T(8,128)S(1)} %copy.251, f32[9,384,35]{2,0,1:T(8,128)} %copy.314, f32[9,384,35]{2,0,1:T(8,128)} %copy.299, f32[9,35,384]{1,0,2:T(8,128)} %copy-done.5, f32[3,9,35,384]{2,1,0,3:T(8,128)} %copy.291, f32[3,9,9,384]{2,1,0,3:T(8,128)} %copy.236, pred[384]{0:T(512)(128)(4,1)S(1)} %get-tuple-element.26, ...), kind=kOutput, calls=%fused_computation.24 | convolution fusion | flops 39795840 | bytes 4244736 | tf_op jit(solution)/shard_map/dpqe,dqbe->pbe/dot_general | solution.py:43
  (132 shorter events, 158.2 us)
Async XLA Ops:
  0.0 11.7 %copy-start = (f32[3,35,35]{2,1,0:T(8,128)S(1)}, f32[3,35,35]{2,1,0:T(8,128)}, u32[]{:S(2)}) copy-start(f32[3,35,35]{2,1,0:T(8,128)} %param.24) | copy-start | bytes 44104
  37.4 1.7 copy-start.2
  64.8 1.7 copy-start.3
  92.3 1.8 copy-start.4
  127.2 22.6 %copy-start.14 = (s32[4,384]{1,0:T(4,128)S(1)}, s32[4,384]{1,0:T(4,128)}, u32[]{:S(2)}) copy-start(s32[4,384]{1,0:T(4,128)} %param.21) | copy-start | bytes 18436
  127.2 22.6 %copy-start.15 = (s32[4,384]{1,0:T(4,128)S(1)}, s32[4,384]{1,0:T(4,128)}, u32[]{:S(2)}) copy-start(s32[4,384]{1,0:T(4,128)} %param.22) | copy-start | bytes 18436
  130.3 26.6 %copy-start.11 = (f32[4,15,35]{2,0,1:T(4,128)S(1)}, f32[4,15,35]{2,0,1:T(4,128)}, u32[]{:S(2)}) copy-start(f32[4,15,35]{2,0,1:T(4,128)} %param.25) | copy-start | bytes 25204
  130.3 102.7 %collective-permute-start = (f32[9,35,32]{1,2,0:T(8,128)}, f32[9,35,32]{1,2,0:T(8,128)}, u32[]{:S(2)}, u32[]{:S(2)}) collective-permute-start(f32[9,35,32]{1,2,0:T(8,128)} %get-tuple-element.22), channel_id=1, source_target_pairs={{4,0},{5,1},{6,2},{7,3},{8,4},{9,5},{10,6},{11,7},{12,8},{13,9},{1... | collective-permute-start | bytes 120968 | tf_op jit(solution)/shard_map/ppermute | solution.py:18
  138.7 98.9 %collective-permute-start.1 = (f32[9,35,32]{1,2,0:T(8,128)}, f32[9,35,32]{1,2,0:T(8,128)}, u32[]{:S(2)}, u32[]{:S(2)}) collective-permute-start(f32[9,35,32]{1,2,0:T(8,128)} %get-tuple-element.21), channel_id=1, source_target_pairs={{3,0},{4,1},{5,2},{6,3},{7,4},{8,5},{9,6},{10,7},{11,8},{12,9},{13... | collective-permute-start | bytes 120968 | tf_op jit(solution)/shard_map/ppermute | solution.py:18
  142.3 99.3 %collective-permute-start.2 = (f32[9,35,32]{1,2,0:T(8,128)}, f32[9,35,32]{1,2,0:T(8,128)}, u32[]{:S(2)}, u32[]{:S(2)}) collective-permute-start(f32[9,35,32]{1,2,0:T(8,128)} %get-tuple-element.20), channel_id=1, source_target_pairs={{2,0},{3,1},{4,2},{5,3},{6,4},{7,5},{8,6},{9,7},{10,8},{11,9},{12,... | collective-permute-start | bytes 120968 | tf_op jit(solution)/shard_map/ppermute | solution.py:18
  144.2 102.4 %collective-permute-start.3 = (f32[9,35,32]{1,2,0:T(8,128)}, f32[9,35,32]{1,2,0:T(8,128)}, u32[]{:S(2)}, u32[]{:S(2)}) collective-permute-start(f32[9,35,32]{1,2,0:T(8,128)} %get-tuple-element.19), channel_id=1, source_target_pairs={{1,0},{2,1},{3,2},{4,3},{5,4},{6,5},{7,6},{8,7},{9,8},{10,9},{11,1... | collective-permute-start | bytes 120968 | tf_op jit(solution)/shard_map/ppermute | solution.py:18
  147.7 99.9 %collective-permute-start.4 = (f32[9,35,32]{1,2,0:T(8,128)}, f32[9,35,32]{1,2,0:T(8,128)}, u32[]{:S(2)}, u32[]{:S(2)}) collective-permute-start(f32[9,35,32]{1,2,0:T(8,128)} %get-tuple-element.18), channel_id=1, source_target_pairs={{0,1},{1,2},{2,3},{3,4},{4,5},{5,6},{6,7},{7,8},{8,9},{9,10},{10,1... | collective-permute-start | bytes 120968 | tf_op jit(solution)/shard_map/ppermute | solution.py:18
  202.0 9.4 %copy-start.17 = (s32[384]{0:T(512)S(1)}, s32[384]{0:T(512)}, u32[]{:S(2)}) copy-start(s32[384]{0:T(512)} %param.20) | copy-start | bytes 4612
  202.0 10.0 %copy-start.12 = (f32[4,35,15]{1,0,2:T(4,128)S(1)}, f32[4,35,15]{1,0,2:T(4,128)}, u32[]{:S(2)}) copy-start(f32[4,35,15]{1,0,2:T(4,128)} %param.26) | copy-start | bytes 25204
  233.0 21.4 %copy-start.1 = (f32[9,35,384]{1,0,2:T(8,128)S(1)}, f32[9,35,384]{1,0,2:T(8,128)}, u32[]{:S(2)}) copy-start(f32[9,35,384]{1,0,2:T(8,128)} %get-tuple-element.27) | copy-start | bytes 1451524
  233.0 15.5 %collective-permute-start.5 = (f32[9,35,32]{1,2,0:T(8,128)}, f32[9,35,32]{1,2,0:T(8,128)S(1)}, u32[]{:S(2)}, u32[]{:S(2)}) collective-permute-start(f32[9,35,32]{1,2,0:T(8,128)} %get-tuple-element.17), channel_id=1, source_target_pairs={{0,2},{1,3},{2,4},{3,5},{4,6},{5,7},{6,8},{7,9},{8,10},{9,11},{10,... | collective-permute-start | bytes 120968 | tf_op jit(solution)/shard_map/ppermute | solution.py:18
  237.6 11.7 %collective-permute-start.6 = (f32[9,35,32]{1,2,0:T(8,128)}, f32[9,35,32]{1,2,0:T(8,128)S(1)}, u32[]{:S(2)}, u32[]{:S(2)}) collective-permute-start(f32[9,35,32]{1,2,0:T(8,128)} %get-tuple-element.16), channel_id=1, source_target_pairs={{0,3},{1,4},{2,5},{3,6},{4,7},{5,8},{6,9},{7,10},{8,11},{9,12},{10... | collective-permute-start | bytes 120968 | tf_op jit(solution)/shard_map/ppermute | solution.py:18
  241.6 12.0 %collective-permute-start.7 = (f32[9,35,32]{1,2,0:T(8,128)S(1)}, f32[9,35,32]{1,2,0:T(8,128)S(1)}, u32[]{:S(2)}, u32[]{:S(2)}) collective-permute-start(f32[9,35,32]{1,2,0:T(8,128)S(1)} %get-tuple-element.15), channel_id=1, source_target_pairs={{0,4},{1,5},{2,6},{3,7},{4,8},{5,9},{6,10},{7,11},{8,12},{9,13},{1... | collective-permute-start | bytes 120968 | tf_op jit(solution)/shard_map/ppermute | solution.py:18
  276.5 4.9 copy-start.13
  350.5 1.6 copy-start.5
  377.8 1.7 copy-start.7
  405.3 1.7 copy-start.8
  432.6 1.6 copy-start.9
  529.0 5.4 copy-start.10
  532.1 28.7 %collective-permute-start.8 = (f32[9,35,32]{1,2,0:T(8,128)}, f32[9,35,32]{1,2,0:T(8,128)}, u32[]{:S(2)}, u32[]{:S(2)}) collective-permute-start(f32[9,35,32]{1,2,0:T(8,128)} %get-tuple-element.14), channel_id=1, source_target_pairs={{4,0},{5,1},{6,2},{7,3},{8,4},{9,5},{10,6},{11,7},{12,8},{13,9},{1... | collective-permute-start | bytes 120968 | tf_op jit(solution)/shard_map/ppermute | solution.py:18
  546.4 34.1 %copy-start.6 = (f32[9,35,384]{1,0,2:T(8,128)S(1)}, f32[9,35,384]{1,0,2:T(8,128)}, u32[]{:S(2)}) copy-start(f32[9,35,384]{1,0,2:T(8,128)} %fusion.19) | copy-start | bytes 1451524
  546.4 18.7 %collective-permute-start.9 = (f32[9,35,32]{1,2,0:T(8,128)}, f32[9,35,32]{1,2,0:T(8,128)S(1)}, u32[]{:S(2)}, u32[]{:S(2)}) collective-permute-start(f32[9,35,32]{1,2,0:T(8,128)} %get-tuple-element.13), channel_id=1, source_target_pairs={{3,0},{4,1},{5,2},{6,3},{7,4},{8,5},{9,6},{10,7},{11,8},{12,9},{13... | collective-permute-start | bytes 120968 | tf_op jit(solution)/shard_map/ppermute | solution.py:18
  553.3 14.1 %collective-permute-start.10 = (f32[9,35,32]{1,2,0:T(8,128)}, f32[9,35,32]{1,2,0:T(8,128)S(1)}, u32[]{:S(2)}, u32[]{:S(2)}) collective-permute-start(f32[9,35,32]{1,2,0:T(8,128)} %get-tuple-element.12), channel_id=1, source_target_pairs={{2,0},{3,1},{4,2},{5,3},{6,4},{7,5},{8,6},{9,7},{10,8},{11,9},{12,... | collective-permute-start | bytes 120968 | tf_op jit(solution)/shard_map/ppermute | solution.py:18
  555.2 16.8 %collective-permute-start.11 = (f32[9,35,32]{1,2,0:T(8,128)}, f32[9,35,32]{1,2,0:T(8,128)S(1)}, u32[]{:S(2)}, u32[]{:S(2)}) collective-permute-start(f32[9,35,32]{1,2,0:T(8,128)} %get-tuple-element.11), channel_id=1, source_target_pairs={{1,0},{2,1},{3,2},{4,3},{5,4},{6,5},{7,6},{8,7},{9,8},{10,9},{11,1... | collective-permute-start | bytes 120968 | tf_op jit(solution)/shard_map/ppermute | solution.py:18
  557.5 14.5 %collective-permute-start.12 = (f32[9,35,32]{1,2,0:T(8,128)}, f32[9,35,32]{1,2,0:T(8,128)S(1)}, u32[]{:S(2)}, u32[]{:S(2)}) collective-permute-start(f32[9,35,32]{1,2,0:T(8,128)} %get-tuple-element.10), channel_id=1, source_target_pairs={{0,1},{1,2},{2,3},{3,4},{4,5},{5,6},{6,7},{7,8},{8,9},{9,10},{10,1... | collective-permute-start | bytes 120968 | tf_op jit(solution)/shard_map/ppermute | solution.py:18
  560.8 11.5 %collective-permute-start.13 = (f32[9,35,32]{1,2,0:T(8,128)}, f32[9,35,32]{1,2,0:T(8,128)S(1)}, u32[]{:S(2)}, u32[]{:S(2)}) collective-permute-start(f32[9,35,32]{1,2,0:T(8,128)} %get-tuple-element.9), channel_id=1, source_target_pairs={{0,2},{1,3},{2,4},{3,5},{4,6},{5,7},{6,8},{7,9},{8,10},{9,11},{10,... | collective-permute-start | bytes 120968 | tf_op jit(solution)/shard_map/ppermute | solution.py:18
  565.1 14.6 %collective-permute-start.14 = (f32[9,35,32]{1,2,0:T(8,128)}, f32[9,35,32]{1,2,0:T(8,128)S(1)}, u32[]{:S(2)}, u32[]{:S(2)}) collective-permute-start(f32[9,35,32]{1,2,0:T(8,128)} %get-tuple-element.8), channel_id=1, source_target_pairs={{0,3},{1,4},{2,5},{3,6},{4,7},{5,8},{6,9},{7,10},{8,11},{9,12},{10... | collective-permute-start | bytes 120968 | tf_op jit(solution)/shard_map/ppermute | solution.py:18
  567.4 12.4 %collective-permute-start.15 = (f32[9,35,32]{1,2,0:T(8,128)S(1)}, f32[9,35,32]{1,2,0:T(8,128)S(1)}, u32[]{:S(2)}, u32[]{:S(2)}) collective-permute-start(f32[9,35,32]{1,2,0:T(8,128)S(1)} %get-tuple-element.6), channel_id=1, source_target_pairs={{0,4},{1,5},{2,6},{3,7},{4,8},{5,9},{6,10},{7,11},{8,12},{9,13},{1... | collective-permute-start | bytes 120968 | tf_op jit(solution)/shard_map/ppermute | solution.py:18
  655.7 5.9 copy-start.16
where the time goes:
time: 696 us; the launch traced here: 683 us
  matrix products  338 us (49%)
  local copies, waits for them, and re-layouts  257 us (37%)
  starting transfers between devices  57.1 us (8%)
  other arithmetic  17.5 us (3%)
  waiting for transfers between devices  12.9 us (2%)
    dot_general x8, matrix products, derivatives(): current = -jnp.einsum('dpqe,dqbe->pbe', star, spread, precision=HIGH)  130 us
    transpose x8, local copies, waits for them, and re-layouts, derivatives(): spread = jnp.einsum('dbc,qce->dqbe', stiffness, current, precision=HIGH)  57.9 us
    ppermute x16, starting transfers between devices, passed_along(): lax.ppermute(value, axis, [(source, source + steps) for source in range(f...  57.1 us
    dot_general x2, matrix products, update(): local = jnp.einsum('ipqe,iqge->ipge', minus, local, precision=HIGH)  52.3 us
    dot_general x2, matrix products, update(): remote = jnp.einsum('ipqe,iqge->ipge', plus, chosen, precision=HIGH)  52.3 us
    unnamed x54, local copies, waits for them, and re-layouts  42.1 us
    gather x4, local copies, waits for them, and re-layouts, beside_all(): return jnp.moveaxis(jnp.take(extended, rows, axis=2), 2, 0)  38.9 us
    dot_general x2, matrix products, update(): volume = jnp.einsum('dpqe,dqbe->pbe', star, spread, precision=HIGH)  34.8 us
  transfers between devices with their start and end apart: 16, of which 4 were waited for; matrix products, arithmetic and copies ran while one was open for 15% of the time, Pallas kernels for 0%

commit v1 on v0

v1 whole, which is shorter than its diff:
```python
import math

import jax
import jax.numpy as jnp
from jax import lax
from jax.experimental import pallas as pl
from jax.experimental.pallas import tpu as pltpu
from jax.sharding import PartitionSpec as P

ORDER = 5
E = 384
F = 128
Q = 9
C = 40
G = 16
GHOST = 256
LANES = 128

HIGH = lax.Precision.HIGHEST
F32 = jnp.float32
BF16 = jnp.bfloat16


def iota(shape, dim):
    return lax.broadcasted_iota(jnp.int32, shape, dim)


def exact(a, b, dims=(((1,), (0,)), ((), ()))):
    return lax.dot_general(a, b, dims, precision=HIGH, preferred_element_type=F32)


def mxu(a, b, dims=(((1,), (0,)), ((), ()))):
    return lax.dot_general(a, b, dims, preferred_element_type=F32)


def split(x):
    high = x.astype(BF16)
    return high, (x - high.astype(F32)).astype(BF16)


def lane_gather(x, at):
    numbers = lax.GatherDimensionNumbers(
        offset_dims=(),
        collapsed_slice_dims=(1,),
        start_index_map=(1,),
        operand_batching_dims=(0,),
        start_indices_batching_dims=(0,),
    )
    mode = lax.GatherScatterMode.PROMISE_IN_BOUNDS
    return lax.gather(x, at[..., None], numbers, (1, 1), mode=mode)


def lanes_of(width):
    return [slice(at, at + LANES) for at in range(0, width, LANES)]


def stiffness_rows(stiffness, transposed, sign, pad_ref):
    total = jnp.zeros((35, 256), F32)
    for d in range(3):
        place = (iota((35, 256), 1) % 128 == d * C + iota((35, 256), 0)).astype(F32)
        dims = (((0,), (0,)), ((), ())) if transposed else (((1,), (0,)), ((), ()))
        total = total + exact(stiffness[d], place, dims)
    pad_ref[32:C, :] = jnp.zeros((8, 256), F32)
    pad_ref[0:35, :] = total * sign
    padded = pad_ref[...]
    high, low = split(padded)
    low = jnp.where(iota((C, 256), 1) < 128, low.astype(F32), 0.0)
    return jnp.concatenate([high.astype(F32), low], axis=0).astype(BF16)


def three(rows, first):
    high, low = split(rows)
    keep = iota(rows.shape, 1) < first
    return jnp.where(keep, high.astype(F32), low.astype(F32)).astype(BF16)


def three_parts(x):
    high, low = split(x)
    return jnp.concatenate([high, low, high], axis=0)


def padded48(x):
    return jnp.concatenate([x, jnp.zeros((8, x.shape[1]), F32)], axis=0)


def star_times(star_ref, source, p, width):
    columns = []
    for at in lanes_of(width):
        values = [source[q, :, at] for q in range(Q)]
        parts = []
        for d in range(3):
            total = star_ref[d, p, 0:1, at] * values[0]
            for q in range(1, Q):
                total = total + star_ref[d, p, q : q + 1, at] * values[q]
            parts.append(total)
        parts.append(jnp.zeros((8, LANES), F32))
        high, low = split(jnp.concatenate(parts, axis=0))
        columns.append(jnp.concatenate([high, low], axis=0))
    return jnp.concatenate(columns, axis=1) if len(columns) > 1 else columns[0]


def halves(out):
    return out[:C] + out[C:]


def taylor(star_ref, rows, cur_ref, width, add):
    for level in range(ORDER - 1):
        source, target = cur_ref.at[level % 2], cur_ref.at[(level + 1) % 2]

        @pl.loop(0, Q)
        def _(p):
            value = halves(mxu(rows, star_times(star_ref, source, p, width)))
            target[p] = value
            add(level, p, value)


def flux(coefficients, source, target, width, accumulate):
    @pl.loop(0, 4)
    def _(i):
        rows = pl.ds(pl.multiple_of(i * G, G), G)
        for at in lanes_of(width):
            values = [source[q, rows, at] for q in range(Q)]
            for p in range(Q):
                total = coefficients[i, p, 0:1, at] * values[0]
                for q in range(1, Q):
                    total = total + coefficients[i, p, q : q + 1, at] * values[q]
                if accumulate:
                    total = target[p, rows, at] + total
                target[p, rows, at] = total


def own_faces(own, proj_rows, face_ref, width):
    @pl.loop(0, Q)
    def _(q):
        face_ref[q] = mxu(proj_rows, three_parts(padded48(own[q])))


def near_faces(parts, neighbour, codes, turn_rows, near_ref, face_ref, width):
    for i in range(4):
        total = None
        wanted = neighbour[i : i + 1, :]
        for arrays, first, mask in parts:
            columns = arrays[0].shape[1]
            hit = iota((columns, width), 0) + first == wanted
            if mask is not None:
                hit = hit & mask
            pick = jnp.where(hit, 1.0, 0.0).astype(BF16)
            for array in arrays:
                piece = mxu(array, pick)
                total = piece if total is None else total + piece
        near_ref[...] = total
        code = codes[i : i + 1, :]

        @pl.loop(0, Q)
        def _(q):
            rows = pl.ds(pl.multiple_of(q * C, 8), C)
            every = mxu(turn_rows, three_parts(padded48(near_ref[rows, :])))
            chosen = every[0:G]
            for k in range(1, 12):
                chosen = jnp.where(code == k, every[k * G : (k + 1) * G], chosen)
            face_ref[q, i * G : (i + 1) * G, :] = chosen


def flat(x):
    return x.reshape(Q * C, x.shape[-1])


def first_kernel(core, dofs, star, stiffness, send_list, early, later, inner, outer, cur, pad):
    for q in range(Q):
        cur[0, q, 32:C, :] = jnp.zeros((8, E), F32)
        cur[0, q, 0:35, :] = dofs[q]
        early[q] = cur[0, q]
        later[q] = cur[0, q]
    rows = stiffness_rows(stiffness, False, -1.0, pad)

    def add(level, p, value):
        k = level + 1
        early[p] = early[p] + value * (1.0 / math.factorial(k + 1))
        later[p] = later[p] + value * ((2.0 ** (k + 1) - 1.0) / math.factorial(k + 1))

    taylor(star, rows, cur, E, add)
    pick = send_pick(core, send_list)
    high, low = split(flat(early[...]))
    sent = mxu(high, pick) + mxu(low, pick)
    inner[...] = sent[:, :LANES]
    outer[...] = sent[:, LANES:]


def send_pick(core, send_list):
    spread = (iota((32, GHOST), 0) == iota((32, GHOST), 1) % 32).astype(F32)
    table = exact(send_list[...].astype(F32), spread)
    message = iota((8, GHOST), 1) // 32
    row = jnp.where(message < 4, 3 - message, jnp.where(message == 4, 4, 12 - message))
    row = jnp.where(core[0] == 0, row, 7 - row)
    wanted = jnp.sum(jnp.where(row == iota((8, GHOST), 0), table, 0.0), axis=0, keepdims=True)
    wanted = wanted.astype(jnp.int32)
    return jnp.where(iota((E, GHOST), 0) == wanted, 1.0, 0.0).astype(BF16)


def ghost_columns(core, neighbour):
    ghost = neighbour - E
    o = ghost >> 5
    offset = jnp.where(o < 4, o - 4, o - 3)
    offset = jnp.where(core[0] == 0, offset, -offset)
    place = jnp.where(offset > 0, (5 - offset) & 3, 3 - offset)
    return jnp.where(neighbour < E, neighbour, E + place * 32 + (ghost & 31))


def fast_rows(cluster):
    fast = cluster == 0
    before = (iota((E, E), 0) < iota((E, E), 1)).astype(F32).astype(BF16)
    rank = mxu(jnp.where(fast, 1.0, 0.0).astype(BF16), before).astype(jnp.int32)
    return jnp.where((iota((F, E), 0) == rank) & fast, 1.0, 0.0).astype(BF16)


def second_kernel(
    core, dofs, star, minus, plus, cluster, neighbour, codes, early,
    stiffness, proj, lift, turn,
    field, star_f, plus_f, lines_f, scatter, nb_all, volume_rows, lift_rows, turn_rows, proj_rows,
    minus_f, early_f, face, flow, near, pad, pad_lift, pad_turn,
):
    volume_rows[...] = stiffness_rows(stiffness, True, 1.0, pad)
    pad_lift[32:C, :] = jnp.zeros((8, 192), F32)
    total = jnp.zeros((35, 192), F32)
    for i in range(4):
        place = (iota((15, 192), 1) % 64 == i * G + iota((15, 192), 0)).astype(F32)
        total = total - exact(lift[i], place)
    pad_lift[0:35, :] = total
    lift_rows[...] = three(pad_lift[...], 128)
    place = (iota((35, 144), 1) % 48 == iota((35, 144), 0)).astype(F32)
    pad_turn[...] = jnp.zeros((192, 144), F32)
    for i in range(4):
        pad_turn[i * G : i * G + 15, :] = exact(proj[i], place)
    proj_rows[...] = three(pad_turn[0:64, :], 96)
    projs = [exact(proj[i], place) for i in range(4)]
    for i in range(4):
        for h in range(3):
            at = (3 * i + h) * G
            pad_turn[at : at + 15, :] = exact(turn[h], projs[i])
    turn_rows[...] = three(pad_turn[...], 96)

    kinds = cluster[...]
    picks = fast_rows(kinds)
    scatter[...] = picks
    column = iota((8, E), 1)
    which = jnp.where(iota((8, E), 0) == 0, column // LANES, column % LANES).astype(F32).astype(BF16)
    found = mxu(which, picks, (((1,), (1,)), ((), ()))).astype(jnp.int32)
    block, lane = found[0:1], found[1:2]

    def take(x):
        r = x.shape[0]
        at = jnp.broadcast_to(lane, (r, F))
        got = [lane_gather(x[:, s], at) for s in lanes_of(E)]
        return jnp.where(block == 0, got[0], jnp.where(block == 1, got[1], got[2]))

    for q in range(Q):
        field[q, 32:C, :] = jnp.zeros((8, F), F32)
        field[q, 0:32, :] = take(dofs[q, 0:32, :])
        field[q, 32:35, :] = take(dofs[q, 32:35, :])
        early_f[q] = take(early[q])

    @pl.loop(0, Q)
    def _(p):
        for d in range(3):
            star_f[d, p, 0:8, :] = take(star[d, p, 0:8, :])
            star_f[d, p, 8:9, :] = take(star[d, p, 8:9, :])
        for i in range(4):
            minus_f[i, p, 0:8, :] = take(minus[i, p, 0:8, :])
            minus_f[i, p, 8:9, :] = take(minus[i, p, 8:9, :])
            plus_f[i, p, 0:8, :] = take(plus[i, p, 0:8, :])
            plus_f[i, p, 8:9, :] = take(plus[i, p, 8:9, :])

    table = ghost_columns(core, neighbour[...])
    nb_all[...] = table
    nb = take(table)
    code = take(codes[...])
    lines_f[0:4, :] = nb
    lines_f[4:8, :] = code

    own_faces(early_f, proj_rows[...], face, F)
    flux(minus_f, face, flow, F, False)
    near_faces([(split(flat(early[...])), 0, None)], nb, code, turn_rows[...], near, face, F)
    flux(plus_f, face, flow, F, True)

    @pl.loop(0, Q)
    def _(p):
        field[p] = (
            field[p]
            + halves(mxu(volume_rows[...], star_times(star_f, early_f, p, F)))
            + mxu(lift_rows[...], three_parts(flow[p]))
        )


def third_kernel(
    core, stiffness, send_list, a, b, q_in, field, star_f, plus_f, lines_f, scatter, cluster, later, dofs,
    lift_rows, turn_rows,
    moved, late, inner, outer,
    late_f, cur, face, flow, near, pad,
):
    ghosts = ghost_array(a, b, q_in)
    near_faces([(split(ghosts), E, None)], lines_f[0:4, :], lines_f[4:8, :], turn_rows[...], near, face, F)
    flux(plus_f, face, flow, F, False)
    for p in range(Q):
        value = field[p] + mxu(lift_rows[...], three_parts(flow[p]))
        cur[0, p] = value
        late_f[0, p] = value
        late_f[1, p] = value
    rows = stiffness_rows(stiffness, False, -1.0, pad)

    def add(level, p, value):
        late_f[0, p] = late_f[0, p] + value * (1.0 / math.factorial(level + 2))

    taylor(star_f, rows, cur, F, add)
    fast = cluster[...] == 0
    picks = scatter[...]
    for p in range(Q):
        high, low = split(late_f[0, p])
        late[p] = jnp.where(fast, mxu(high, picks) + mxu(low, picks), later[p])
    pick = send_pick(core, send_list)
    high, low = split(flat(late[...]))
    sent = mxu(high, pick) + mxu(low, pick)
    inner[...] = sent[:, :LANES]
    outer[...] = sent[:, LANES:]
    for p in range(Q):
        moved[p] = late_f[1, p]


def ghost_array(a, b, q_in):
    part = iota((Q * C, LANES), 1) // 32
    mine = jnp.where((part == 0) | (part == 3), a[...], b[...])
    return jnp.concatenate([mine, q_in[...]], axis=1)


def fourth_kernel(
    dofs, star, minus, plus, cluster, nb_all, codes, early, later, late, moved, scatter,
    a, b, q_in, volume_rows, lift_rows, turn_rows, proj_rows,
    out, own, face, flow, near,
):
    kinds = cluster[...]
    fast = kinds == 0
    picks = scatter[...]
    for p in range(Q):
        own[p] = jnp.where(fast, late[p], early[p] + later[p])
        high, low = split(moved[p])
        out[p] = jnp.where(fast, mxu(high, picks) + mxu(low, picks), 0.0)
        out[p, 0:35, :] = jnp.where(fast, out[p, 0:35, :], dofs[p])
    own_faces(own, proj_rows[...], face, E)
    flux(minus, face, flow, E, False)
    ghosts = ghost_array(a, b, q_in)
    near_faces(
        [
            (split(flat(late[...])), 0, None),
            (split(flat(early[...])), 0, kinds == 1),
            (split(ghosts), E, kinds == 1),
        ],
        nb_all[...], codes[...], turn_rows[...], near, face, E,
    )
    flux(plus, face, flow, E, True)

    @pl.loop(0, Q)
    def _(p):
        out[p] = (
            out[p]
            + halves(mxu(volume_rows[...], star_times(star, own, p, E)))
            + mxu(lift_rows[...], three_parts(flow[p]))
        )


def fifth_kernel(
    dofs, plus, cluster, nb_all, codes, partial, a, b, q_in, lift_rows, turn_rows,
    out, face, flow, near,
):
    ghosts = ghost_array(a, b, q_in)
    near_faces([(split(ghosts), E, None)], nb_all[...], codes[...], turn_rows[...], near, face, E)
    flux(plus, face, flow, E, False)
    active = cluster[...] < 2
    for p in range(Q):
        value = partial[p] + mxu(lift_rows[...], three_parts(flow[p]))
        out[p] = jnp.where(active, value[0:35], dofs[p])


def call(kernel, outs, args, scratch, scalars=0):
    vmem = pl.BlockSpec(memory_space=pltpu.VMEM)
    smem = pl.BlockSpec(memory_space=pltpu.SMEM)
    return pl.pallas_call(
        kernel,
        out_shape=[jax.ShapeDtypeStruct(*o) for o in outs],
        in_specs=[smem] * scalars + [vmem] * (len(args) - scalars),
        out_specs=[vmem] * len(outs),
        scratch_shapes=[pltpu.VMEM(*s) for s in scratch],
        compiler_params=pltpu.CompilerParams(vmem_limit_bytes=48 * 1024 * 1024),
        name=kernel.__name__,
    )(*args)


def exchange(inner, outer):
    count = lax.axis_size("dom")
    chips = count // 2

    def along(reach):
        def target(device):
            chip, core = device // 2, device % 2
            return 2 * ((chip + (reach if core == 0 else -reach)) % chips) + core

        return [(device, target(device)) for device in range(count)]

    pair = [(device, device ^ 1) for device in range(count)]
    part = iota((1, LANES), 1) // 32
    beside = lax.ppermute(inner, "dom", pair)
    a = lax.ppermute(jnp.where(part < 2, beside, outer), "dom", along(1))
    b = lax.ppermute(jnp.where(part < 2, outer, beside), "dom", along(2))
    back = jnp.where(part == 0, outer, jnp.where(part == 3, b, a))
    return a, b, lax.ppermute(back, "dom", pair)


def body(
    dofs,
    star,
    flux_minus,
    flux_plus,
    cluster,
    neighbour,
    face_code,
    send_list,
    stiffness,
    face_proj,
    face_lift,
    face_turn,
):
    core = (lax.axis_index("dom") % 2).astype(jnp.int32).reshape(1)
    cluster = cluster.reshape(1, E)
    whole, compact, block = (Q, C, E), (Q, C, F), (Q * C, LANES)
    early, later, inner, outer = call(
        first_kernel,
        [(whole, F32), (whole, F32), (block, F32), (block, F32)],
        [core, dofs, star, stiffness, send_list],
        [((2,) + whole, F32), ((C, 256), F32)],
        1,
    )
    a, b, q_in = exchange(inner, outer)
    (
        field, star_f, plus_f, lines_f, scatter, nb_all, volume_rows, lift_rows, turn_rows, proj_rows
    ) = call(
        second_kernel,
        [
            (compact, F32), ((3, Q, Q, F), F32), ((4, Q, Q, F), F32), ((8, F), jnp.int32),
            ((F, E), BF16), ((4, E), jnp.int32),
            ((2 * C, 256), BF16), ((C, 192), BF16), ((192, 144), BF16), ((64, 144), BF16),
        ],
        [
            core, dofs, star, flux_minus, flux_plus, cluster, neighbour, face_code, early,
            stiffness, face_proj, face_lift, face_turn,
        ],
        [
            ((4, Q, Q, F), F32), (compact, F32), ((Q, 64, F), F32), ((Q, 64, F), F32),
            ((Q * C, F), F32), ((C, 256), F32), ((C, 192), F32), ((192, 144), F32),
        ],
        1,
    )
    moved, late, inner, outer = call(
        third_kernel,
        [(compact, F32), (whole, F32), (block, F32), (block, F32)],
        [
            core, stiffness, send_list, a, b, q_in, field, star_f, plus_f, lines_f, scatter, cluster,
            later, dofs, lift_rows, turn_rows,
        ],
        [
            ((2,) + compact, F32), ((2,) + compact, F32), ((Q, 64, F), F32), ((Q, 64, F), F32),
            ((Q * C, F), F32), ((C, 256), F32),
        ],
        1,
    )
    a2, b2, q2 = exchange(inner, outer)
    (partial,) = call(
        fourth_kernel,
        [(whole, F32)],
        [
            dofs, star, flux_minus, flux_plus, cluster, nb_all, face_code, early, later, late, moved,
            scatter, a, b, q_in, volume_rows, lift_rows, turn_rows, proj_rows,
        ],
        [(whole, F32), ((Q, 64, E), F32), ((Q, 64, E), F32), ((Q * C, E), F32)],
    )
    (out,) = call(
        fifth_kernel,
        [((Q, 35, E), F32)],
        [dofs, flux_plus, cluster, nb_all, face_code, partial, a2, b2, q2, lift_rows, turn_rows],
        [((Q, 64, E), F32), ((Q, 64, E), F32), ((Q * C, E), F32)],
    )
    return out


def solution(mesh):
    return jax.shard_map(
        body,
        mesh=mesh,
        in_specs=(
            P(None, None, "dom"),
            P(None, None, None, "dom"),
            P(None, None, None, "dom"),
            P(None, None, None, "dom"),
            P("dom"),
            P(None, "dom"),
            P(None, "dom"),
            P(None, "dom"),
            P(),
            P(),
            P(),
            P(),
        ),
        out_specs=P(None, None, "dom"),
        check_vma=False,
    )
```

time: 696 us -> 111 us (0.16)
  the two profiles are of different devices: /device:TPU:25 before, /device:TPU:1 now
where the time goes in v1:
time: 111 us; the launch traced here: 110 us
  Pallas kernels  70.4 us (63%)
  starting transfers between devices  22.2 us (20%)
  waiting for transfers between devices  12.5 us (11%)
  local copies, waits for them, and re-layouts  4.69 us (4%)
    pallas_call x5, Pallas kernels, call(): pl.pallas_call(kernel, out_shape=[jax.ShapeDtypeStruct(*o) for o in outs]...  70.4 us
    ppermute x2, starting transfers between devices, exchange(): b = lax.ppermute(jnp.where(part < 2, outer, beside), 'dom', along(2))  11.6 us
    ppermute x2, waiting for transfers between devices, exchange(): a = lax.ppermute(jnp.where(part < 2, beside, outer), 'dom', along(1))  6.25 us
    ppermute x2, starting transfers between devices, exchange(): return (a, b, lax.ppermute(back, 'dom', pair))  5.78 us
    unnamed x29, local copies, waits for them, and re-layouts  4.69 us
    ppermute x2, waiting for transfers between devices, exchange(): b = lax.ppermute(jnp.where(part < 2, outer, beside), 'dom', along(2))  4.12 us
    ppermute x2, starting transfers between devices, exchange(): a = lax.ppermute(jnp.where(part < 2, beside, outer), 'dom', along(1))  2.65 us
  transfers between devices with their start and end apart: 8, of which 6 were waited for; matrix products, arithmetic and copies ran while one was open for 1% of the time, Pallas kernels for 30%

profile of v1, /device:TPU:1, one launch (start us, length us, event | category | flops | bytes accessed | tf_op | source)
XLA Modules:
  0.0 110.1 jit_solution(13279367518329266171)
XLA Ops:
  0.0 0.0 copy-start.2
  0.0 0.0 copy-start.3
  0.0 1.1 %copy.14.star = f32[3,9,9,384]{3,2,1,0:T(8,128)S(1)} copy(f32[3,9,9,384]{3,0,2,1:T(4,128)} %param.13) | data formatting | bytes 746496 | tf_op args[1]
  1.2 0.0 copy-start.6
  1.2 0.0 copy-done.2
  1.2 0.0 copy-done.3
  1.2 0.7 copy-done.6
  1.9 11.2 %first_kernel.1 = (f32[9,40,384]{2,1,0:T(8,128)S(1)}, f32[9,40,384]{2,1,0:T(8,128)S(1)}, f32[360,128]{1,0:T(8,128)S(1)}, f32[360,128]{1,0:T(8,128)S(1)}) custom-call(s32[1]{0:T(128)} %bitcast.core, f32[9,35,384]{2,1,0:T(8,128)S(1)} %copy-done.2, f32[3,9,9,384]{3,2,1,0:T(8,128)S(1)} %copy.14.star, f32[3,35,35]{2,1,0:T(8,128)S(1)} %copy-done.3, ...), custom_call_target="tpu_custom_call" | custom-call | tf_op jit(solution)/shard_map/first_kernel/pallas_call | solution.py:385
  13.1 1.5 %collective-permute-start = (f32[360,128]{1,0:T(8,128)S(1)}, f32[360,128]{1,0:T(8,128)S(1)}, u32[]{:S(2)}, u32[]{:S(2)}) collective-permute-start(f32[360,128]{1,0:T(8,128)S(1)} %get-tuple-element.26), channel_id=1, source_target_pairs={{0,1},{1,0},{2,3},{3,2},{4,5},{5,4},{6,7},{7,6},{8,9},{9,8},{10,11... | collective-permute-start | bytes 552968 | tf_op jit(solution)/shard_map/ppermute | solution.py:409
  14.6 1.0 collective-permute-done
  15.7 8.8 %collective-permute-start.2 = (f32[360,128]{1,0:T(8,128)S(1)}, f32[360,128]{1,0:T(8,128)S(1)}, u32[]{:S(2)}, u32[]{:S(2)}) collective-permute-start(f32[360,128]{1,0:T(8,128)S(1)} %get-tuple-element.43), channel_id=1, source_target_pairs={{0,4},{1,125},{2,6},{3,127},{4,8},{5,1},{6,10},{7,3},{8,12},{9,5},... | collective-permute-start | bytes 552968 | tf_op jit(solution)/shard_map/ppermute | solution.py:411
  24.5 0.9 collective-permute-start.1
  25.4 1.6 %collective-permute-done.2.b = f32[360,128]{1,0:T(8,128)S(1)} collective-permute-done((f32[360,128]{1,0:T(8,128)S(1)}, f32[360,128]{1,0:T(8,128)S(1)}, u32[]{:S(2)}, u32[]{:S(2)}) %collective-permute-start.2) | collective-permute-done | bytes 184352 | tf_op jit(solution)/shard_map/ppermute | solution.py:411
  27.0 3.0 %collective-permute-done.1.a = f32[360,128]{1,0:T(8,128)S(1)} collective-permute-done((f32[360,128]{1,0:T(8,128)S(1)}, f32[360,128]{1,0:T(8,128)S(1)}, u32[]{:S(2)}, u32[]{:S(2)}) %collective-permute-start.1) | collective-permute-done | bytes 184352 | tf_op jit(solution)/shard_map/ppermute | solution.py:410
  30.0 0.0 copy-start.11
  30.0 0.0 copy-start.9
  30.1 2.4 %collective-permute-start.3 = (f32[360,128]{1,0:T(8,128)S(1)}, f32[360,128]{1,0:T(8,128)S(1)}, u32[]{:S(2)}, u32[]{:S(2)}) collective-permute-start(f32[360,128]{1,0:T(8,128)S(1)} %select_select_fusion.1), channel_id=1, source_target_pairs={{0,1},{1,0},{2,3},{3,2},{4,5},{5,4},{6,7},{7,6},{8,9},{9,8},{10,11... | collective-permute-start | bytes 552968 | tf_op jit(solution)/shard_map/ppermute | solution.py:413
  32.4 0.0 copy-done.11
  32.4 0.0 copy-done.9
  32.4 0.0 copy-start.10
  32.5 0.7 copy-done.10
  33.2 0.1 copy.18.lift
  33.3 1.2 %copy.22.plus = f32[4,9,9,384]{3,2,1,0:T(8,128)S(1)} copy(f32[4,9,9,384]{3,0,2,1:T(4,128)} %param.15) | data formatting | bytes 995328 | tf_op args[3]
  34.5 0.0 copy-done.8
  34.5 0.0 copy-start
  34.5 0.0 copy-start.4
  34.5 0.0 copy-start.5
  34.5 0.0 copy-start.7
  34.5 0.1 copy.15.minus
  34.6 0.6 copy-done.4
  35.2 0.1 copy-done.5
  35.3 0.0 copy-done.7
  35.3 14.6 %second_kernel.1 = (f32[9,40,128]{2,1,0:T(8,128)S(1)}, f32[3,9,9,128]{3,2,1,0:T(8,128)S(1)}, f32[4,9,9,128]{3,2,1,0:T(8,128)S(1)}, s32[8,128]{1,0:T(8,128)S(1)},...) custom-call(s32[1]{0:T(128)} %bitcast.core, ...), custom_call_target="tpu_custom_call" | custom-call | tf_op jit(solution)/shard_map/second_kernel/pallas_call | solution.py:385
  50.0 0.0 copy-done
  50.0 0.0 collective-permute-done.3.q_in
  50.0 15.3 %third_kernel.1 = (f32[9,40,128]{2,1,0:T(8,128)S(1)}, f32[9,40,384]{2,1,0:T(8,128)S(1)}, f32[360,128]{1,0:T(8,128)S(1)}, f32[360,128]{1,0:T(8,128)S(1)}) custom-call(s32[1]{0:T(128)} %bitcast.core, f32[3,35,35]{2,1,0:T(8,128)S(1)} %copy-done.3, s32[8,32]{1,0:T(8,128)S(1)} %copy-done.6, f32[360,128]{1,0:T(8,128)S(1)} %collective-permute-done.1.a, ...), custom_call_target="tpu_custom_call" | custom-call | tf_op jit(solution)/shard_map/third_kernel/pallas_call | solution.py:385
  65.3 0.7 collective-permute-start.4
  66.0 1.1 collective-permute-done.4
  67.1 2.8 %collective-permute-start.6 = (f32[360,128]{1,0:T(8,128)S(1)}, f32[360,128]{1,0:T(8,128)S(1)}, u32[]{:S(2)}, u32[]{:S(2)}) collective-permute-start(f32[360,128]{1,0:T(8,128)S(1)} %get-tuple-element.41), channel_id=1, source_target_pairs={{0,4},{1,125},{2,6},{3,127},{4,8},{5,1},{6,10},{7,3},{8,12},{9,5},... | collective-permute-start | bytes 552968 | tf_op jit(solution)/shard_map/ppermute | solution.py:411
  69.9 1.8 %collective-permute-start.5 = (f32[360,128]{1,0:T(8,128)S(1)}, f32[360,128]{1,0:T(8,128)S(1)}, u32[]{:S(2)}, u32[]{:S(2)}) collective-permute-start(f32[360,128]{1,0:T(8,128)S(1)} %get-tuple-element.42), channel_id=1, source_target_pairs={{0,2},{1,127},{2,4},{3,1},{4,6},{5,3},{6,8},{7,5},{8,10},{9,7},{10... | collective-permute-start | bytes 552968 | tf_op jit(solution)/shard_map/ppermute | solution.py:410
  71.7 2.5 %collective-permute-done.6.b = f32[360,128]{1,0:T(8,128)S(1)} collective-permute-done((f32[360,128]{1,0:T(8,128)S(1)}, f32[360,128]{1,0:T(8,128)S(1)}, u32[]{:S(2)}, u32[]{:S(2)}) %collective-permute-start.6) | collective-permute-done | bytes 184352 | tf_op jit(solution)/shard_map/ppermute | solution.py:411
  74.2 3.2 %collective-permute-done.5.a = f32[360,128]{1,0:T(8,128)S(1)} collective-permute-done((f32[360,128]{1,0:T(8,128)S(1)}, f32[360,128]{1,0:T(8,128)S(1)}, u32[]{:S(2)}, u32[]{:S(2)}) %collective-permute-start.5) | collective-permute-done | bytes 184352 | tf_op jit(solution)/shard_map/ppermute | solution.py:410
  77.4 0.1 select_select_fusion
  77.5 3.4 %collective-permute-start.7 = (f32[360,128]{1,0:T(8,128)S(1)}, f32[360,128]{1,0:T(8,128)S(1)}, u32[]{:S(2)}, u32[]{:S(2)}) collective-permute-start(f32[360,128]{1,0:T(8,128)S(1)} %select_select_fusion), channel_id=1, source_target_pairs={{0,1},{1,0},{2,3},{3,2},{4,5},{5,4},{6,7},{7,6},{8,9},{9,8},{10,11... | collective-permute-start | bytes 552968 | tf_op jit(solution)/shard_map/ppermute | solution.py:413
  80.9 18.8 %fourth_kernel.1.partial = f32[9,40,384]{2,1,0:T(8,128)S(1)} custom-call(f32[9,35,384]{2,1,0:T(8,128)S(1)} %copy-done.2, f32[3,9,9,384]{3,2,1,0:T(8,128)S(1)} %copy.14.star, f32[4,9,9,384]{3,2,1,0:T(8,128)S(1)} %copy.15.minus, f32[4,9,9,384]{3,2,1,0:T(8,128)} %copy-done, s32[1,384]{1,0:T(1,128)S(1)} %reshape.51.cluster, ...), custom_call_target="tpu_custom_call" | custom-call | tf_op jit(solution)/shard_map/fourth_kernel/pallas_call | solution.py:385
  99.7 0.0 collective-permute-done.7.q_in
  99.7 0.0 copy-done.1
  99.7 10.4 %fifth_kernel.1 = f32[9,35,384]{2,1,0:T(8,128)} custom-call(f32[9,35,384]{2,1,0:T(8,128)S(1)} %copy-done.2, f32[4,9,9,384]{3,2,1,0:T(8,128)S(1)} %copy-done.1, s32[1,384]{1,0:T(1,128)S(1)} %reshape.51.cluster, s32[4,384]{1,0:T(4,128)S(1)} %get-tuple-element.24.nb_all, s32[4,384]{1,0:T(4,128)S(1)} %copy-done.4, f32[9,40,384]{2,1,0:T(8,128)S(1)} %fourth_kernel.1.partial, ...), custom_call_target="tpu_custom_call" | custom-call | tf_op jit(solution)/shard_map/fifth_kernel/pallas_call | solution.py:385
  (9 shorter events, 0.1 us)
Async XLA Ops:
  0.0 1.2 %copy-start.2 = (f32[9,35,384]{2,1,0:T(8,128)S(1)}, f32[9,35,384]{2,1,0:T(8,128)}, u32[]{:S(2)}) copy-start(f32[9,35,384]{2,1,0:T(8,128)} %dofs.9) | copy-start | bytes 1451524
  0.0 1.2 %copy-start.3 = (f32[3,35,35]{2,1,0:T(8,128)S(1)}, f32[3,35,35]{2,1,0:T(8,128)}, u32[]{:S(2)}) copy-start(f32[3,35,35]{2,1,0:T(8,128)} %stiffness.5) | copy-start | bytes 44104
  1.2 0.7 copy-start.6
  13.1 2.6 %collective-permute-start = (f32[360,128]{1,0:T(8,128)S(1)}, f32[360,128]{1,0:T(8,128)S(1)}, u32[]{:S(2)}, u32[]{:S(2)}) collective-permute-start(f32[360,128]{1,0:T(8,128)S(1)} %get-tuple-element.26), channel_id=1, source_target_pairs={{0,1},{1,0},{2,3},{3,2},{4,5},{5,4},{6,7},{7,6},{8,9},{9,8},{10,11... | collective-permute-start | bytes 552968 | tf_op jit(solution)/shard_map/ppermute | solution.py:409
  15.7 11.3 %collective-permute-start.2 = (f32[360,128]{1,0:T(8,128)S(1)}, f32[360,128]{1,0:T(8,128)S(1)}, u32[]{:S(2)}, u32[]{:S(2)}) collective-permute-start(f32[360,128]{1,0:T(8,128)S(1)} %get-tuple-element.43), channel_id=1, source_target_pairs={{0,4},{1,125},{2,6},{3,127},{4,8},{5,1},{6,10},{7,3},{8,12},{9,5},... | collective-permute-start | bytes 552968 | tf_op jit(solution)/shard_map/ppermute | solution.py:411
  24.5 5.5 %collective-permute-start.1 = (f32[360,128]{1,0:T(8,128)S(1)}, f32[360,128]{1,0:T(8,128)S(1)}, u32[]{:S(2)}, u32[]{:S(2)}) collective-permute-start(f32[360,128]{1,0:T(8,128)S(1)} %get-tuple-element.44), channel_id=1, source_target_pairs={{0,2},{1,127},{2,4},{3,1},{4,6},{5,3},{6,8},{7,5},{8,10},{9,7},{10... | collective-permute-start | bytes 552968 | tf_op jit(solution)/shard_map/ppermute | solution.py:410
  30.0 2.4 %copy-start.11 = (s32[384]{0:T(512)S(1)}, s32[384]{0:T(512)}, u32[]{:S(2)}) copy-start(s32[384]{0:T(512)} %param.16) | copy-start | bytes 4612
  30.0 2.4 %copy-start.9 = (f32[4,15,35]{2,0,1:T(4,128)S(1)}, f32[4,15,35]{2,0,1:T(4,128)}, u32[]{:S(2)}) copy-start(f32[4,15,35]{2,0,1:T(4,128)} %param.21) | copy-start | bytes 25204
  30.1 19.9 %collective-permute-start.3 = (f32[360,128]{1,0:T(8,128)S(1)}, f32[360,128]{1,0:T(8,128)S(1)}, u32[]{:S(2)}, u32[]{:S(2)}) collective-permute-start(f32[360,128]{1,0:T(8,128)S(1)} %select_select_fusion.1), channel_id=1, source_target_pairs={{0,1},{1,0},{2,3},{3,2},{4,5},{5,4},{6,7},{7,6},{8,9},{9,8},{10,11... | collective-permute-start | bytes 552968 | tf_op jit(solution)/shard_map/ppermute | solution.py:413
  32.4 0.8 copy-start.10
  33.3 1.2 %copy-start.8 = (f32[4,9,9,384]{3,0,2,1:T(4,128)S(1)}, f32[4,9,9,384]{3,0,2,1:T(4,128)}, u32[]{:S(2)}) copy-start(f32[4,9,9,384]{3,0,2,1:T(4,128)} %param.14) | copy-start | bytes 1492996
  34.5 15.5 %copy-start = (f32[4,9,9,384]{3,2,1,0:T(8,128)}, f32[4,9,9,384]{3,2,1,0:T(8,128)S(1)}, u32[]{:S(2)}) copy-start(f32[4,9,9,384]{3,2,1,0:T(8,128)S(1)} %copy.22.plus) | copy-start | bytes 1492996
  34.5 0.7 copy-start.4
  34.5 0.8 copy-start.5
  34.5 0.8 copy-start.7
  65.3 1.8 %collective-permute-start.4 = (f32[360,128]{1,0:T(8,128)S(1)}, f32[360,128]{1,0:T(8,128)S(1)}, u32[]{:S(2)}, u32[]{:S(2)}) collective-permute-start(f32[360,128]{1,0:T(8,128)S(1)} %get-tuple-element.39), channel_id=1, source_target_pairs={{0,1},{1,0},{2,3},{3,2},{4,5},{5,4},{6,7},{7,6},{8,9},{9,8},{10,11... | collective-permute-start | bytes 552968 | tf_op jit(solution)/shard_map/ppermute | solution.py:409
  67.1 7.1 %collective-permute-start.6 = (f32[360,128]{1,0:T(8,128)S(1)}, f32[360,128]{1,0:T(8,128)S(1)}, u32[]{:S(2)}, u32[]{:S(2)}) collective-permute-start(f32[360,128]{1,0:T(8,128)S(1)} %get-tuple-element.41), channel_id=1, source_target_pairs={{0,4},{1,125},{2,6},{3,127},{4,8},{5,1},{6,10},{7,3},{8,12},{9,5},... | collective-permute-start | bytes 552968 | tf_op jit(solution)/shard_map/ppermute | solution.py:411
  69.9 7.5 %collective-permute-start.5 = (f32[360,128]{1,0:T(8,128)S(1)}, f32[360,128]{1,0:T(8,128)S(1)}, u32[]{:S(2)}, u32[]{:S(2)}) collective-permute-start(f32[360,128]{1,0:T(8,128)S(1)} %get-tuple-element.42), channel_id=1, source_target_pairs={{0,2},{1,127},{2,4},{3,1},{4,6},{5,3},{6,8},{7,5},{8,10},{9,7},{10... | collective-permute-start | bytes 552968 | tf_op jit(solution)/shard_map/ppermute | solution.py:410
  77.5 22.2 %collective-permute-start.7 = (f32[360,128]{1,0:T(8,128)S(1)}, f32[360,128]{1,0:T(8,128)S(1)}, u32[]{:S(2)}, u32[]{:S(2)}) collective-permute-start(f32[360,128]{1,0:T(8,128)S(1)} %select_select_fusion), channel_id=1, source_target_pairs={{0,1},{1,0},{2,3},{3,2},{4,5},{5,4},{6,7},{7,6},{8,9},{9,8},{10,11... | collective-permute-start | bytes 552968 | tf_op jit(solution)/shard_map/ppermute | solution.py:413
  80.9 18.8 %copy-start.1 = (f32[4,9,9,384]{3,2,1,0:T(8,128)S(1)}, f32[4,9,9,384]{3,2,1,0:T(8,128)}, u32[]{:S(2)}) copy-start(f32[4,9,9,384]{3,2,1,0:T(8,128)} %copy-done) | copy-start | bytes 1492996

commit v2 on v1

--- a/solution.py
+++ b/solution.py
@@ -89,9 +89,9 @@
         values = [source[q, :, at] for q in range(Q)]
         parts = []
         for d in range(3):
-            total = star_ref[d, p, 0:1, at] * values[0]
+            total = star_ref[p, 0, d : d + 1, at] * values[0]
             for q in range(1, Q):
-                total = total + star_ref[d, p, q : q + 1, at] * values[q]
+                total = total + star_ref[p, q, d : d + 1, at] * values[q]
             parts.append(total)
         parts.append(jnp.zeros((8, LANES), F32))
         high, low = split(jnp.concatenate(parts, axis=0))
@@ -106,78 +106,93 @@
 def taylor(star_ref, rows, cur_ref, width, add):
     for level in range(ORDER - 1):
         source, target = cur_ref.at[level % 2], cur_ref.at[(level + 1) % 2]
-
-        @pl.loop(0, Q)
-        def _(p):
+        for p in range(Q):
             value = halves(mxu(rows, star_times(star_ref, source, p, width)))
             target[p] = value
             add(level, p, value)
 
 
 def flux(coefficients, source, target, width, accumulate):
-    @pl.loop(0, 4)
-    def _(i):
-        rows = pl.ds(pl.multiple_of(i * G, G), G)
+    for i in range(4):
+        rows = slice(i * G, (i + 1) * G)
         for at in lanes_of(width):
             values = [source[q, rows, at] for q in range(Q)]
             for p in range(Q):
-                total = coefficients[i, p, 0:1, at] * values[0]
+                total = coefficients[p, 0, i : i + 1, at] * values[0]
                 for q in range(1, Q):
-                    total = total + coefficients[i, p, q : q + 1, at] * values[q]
+                    total = total + coefficients[p, q, i : i + 1, at] * values[q]
                 if accumulate:
                     total = target[p, rows, at] + total
                 target[p, rows, at] = total
 
 
 def own_faces(own, proj_rows, face_ref, width):
-    @pl.loop(0, Q)
-    def _(q):
+    for q in range(Q):
         face_ref[q] = mxu(proj_rows, three_parts(padded48(own[q])))
 
 
+def beside(rows):
+    return jnp.concatenate([rows[i : i + 1, :] for i in range(4)], axis=1)
+
+
 def near_faces(parts, neighbour, codes, turn_rows, near_ref, face_ref, width):
-    for i in range(4):
-        total = None
-        wanted = neighbour[i : i + 1, :]
-        for arrays, first, mask in parts:
-            columns = arrays[0].shape[1]
-            hit = iota((columns, width), 0) + first == wanted
-            if mask is not None:
-                hit = hit & mask
-            pick = jnp.where(hit, 1.0, 0.0).astype(BF16)
-            for array in arrays:
-                piece = mxu(array, pick)
-                total = piece if total is None else total + piece
-        near_ref[...] = total
-        code = codes[i : i + 1, :]
-
-        @pl.loop(0, Q)
-        def _(q):
-            rows = pl.ds(pl.multiple_of(q * C, 8), C)
-            every = mxu(turn_rows, three_parts(padded48(near_ref[rows, :])))
-            chosen = every[0:G]
-            for k in range(1, 12):
-                chosen = jnp.where(code == k, every[k * G : (k + 1) * G], chosen)
-            face_ref[q, i * G : (i + 1) * G, :] = chosen
+    total = None
+    wanted = beside(neighbour)
+    for arrays, first, mask in parts:
+        columns = arrays[0].shape[1]
+        hit = iota((columns, 4 * width), 0) + first == wanted
+        if mask is not None:
+            hit = hit & jnp.concatenate([mask] * 4, axis=1)
+        pick = jnp.where(hit, 1.0, 0.0).astype(BF16)
+        for array in arrays:
+            piece = mxu(array, pick)
+            total = piece if total is None else total + piece
+    near_ref[...] = total
+    code = beside(codes)
+    for q in range(Q):
+        every = mxu(turn_rows, three_parts(padded48(near_ref[q * C : (q + 1) * C, :])))
+        chosen = every[0:G]
+        for k in range(1, 12):
+            chosen = jnp.where(code == k, every[k * G : (k + 1) * G], chosen)
+        for i in range(4):
+            face_ref[q, i * G : (i + 1) * G, :] = chosen[:, i * width : (i + 1) * width]
 
 
 def flat(x):
     return x.reshape(Q * C, x.shape[-1])
 
 
-def first_kernel(core, dofs, star, stiffness, send_list, early, later, inner, outer, cur, pad):
+def first_kernel(
+    core, dofs_in, star_in, stiffness_in, send_list_in,
+    early, later, inner, outer,
+    cur, pad, dofs, star, stiffness, send_list, done,
+):
+    small = [
+        pltpu.make_async_copy(stiffness_in, stiffness, done.at[18]),
+        pltpu.make_async_copy(send_list_in, send_list, done.at[19]),
+    ]
+    fields = [pltpu.make_async_copy(dofs_in.at[q], dofs.at[q], done.at[q]) for q in range(Q)]
+    stars = [pltpu.make_async_copy(star_in.at[p], star.at[p], done.at[Q + p]) for p in range(Q)]
+    for copy in small + fields + stars:
+        copy.start()
     for q in range(Q):
         cur[0, q, 32:C, :] = jnp.zeros((8, E), F32)
+    small[0].wait()
+    small[1].wait()
+    rows = stiffness_rows(stiffness, False, -1.0, pad)
+    for q in range(Q):
+        fields[q].wait()
         cur[0, q, 0:35, :] = dofs[q]
         early[q] = cur[0, q]
         later[q] = cur[0, q]
-    rows = stiffness_rows(stiffness, False, -1.0, pad)
 
     def add(level, p, value):
         k = level + 1
         early[p] = early[p] + value * (1.0 / math.factorial(k + 1))
         later[p] = later[p] + value * ((2.0 ** (k + 1) - 1.0) / math.factorial(k + 1))
 
+    for copy in stars:
+        copy.wait()
     taylor(star, rows, cur, E, add)
     pick = send_pick(core, send_list)
     high, low = split(flat(early[...]))
@@ -215,10 +230,11 @@
 
 def second_kernel(
     core, dofs, star, minus, plus, cluster, neighbour, codes, early,
-    stiffness, proj, lift, turn,
-    field, star_f, plus_f, lines_f, scatter, nb_all, volume_rows, lift_rows, turn_rows, proj_rows,
+    stiffness, proj, lift, turn, outer,
+    field, star_f, plus_f, lines_f, scatter, nb_all, volume_rows, lift_rows, turn_rows, proj_rows, kept,
     minus_f, early_f, face, flow, near, pad, pad_lift, pad_turn,
 ):
+    kept[...] = outer[...]
     volume_rows[...] = stiffness_rows(stiffness, True, 1.0, pad)
     pad_lift[32:C, :] = jnp.zeros((8, 192), F32)
     total = jnp.zeros((35, 192), F32)
@@ -261,14 +277,10 @@
 
     @pl.loop(0, Q)
     def _(p):
-        for d in range(3):
-            star_f[d, p, 0:8, :] = take(star[d, p, 0:8, :])
-            star_f[d, p, 8:9, :] = take(star[d, p, 8:9, :])
-        for i in range(4):
-            minus_f[i, p, 0:8, :] = take(minus[i, p, 0:8, :])
-            minus_f[i, p, 8:9, :] = take(minus[i, p, 8:9, :])
-            plus_f[i, p, 0:8, :] = take(plus[i, p, 0:8, :])
-            plus_f[i, p, 8:9, :] = take(plus[i, p, 8:9, :])
+        for q in range(Q):
+            star_f[p, q] = take(star[p, q])
+            minus_f[p, q] = take(minus[p, q])
+            plus_f[p, q] = take(plus[p, q])
 
     table = ghost_columns(core, neighbour[...])
     nb_all[...] = table
@@ -282,8 +294,7 @@
     near_faces([(split(flat(early[...])), 0, None)], nb, code, turn_rows[...], near, face, F)
     flux(plus_f, face, flow, F, True)
 
-    @pl.loop(0, Q)
-    def _(p):
+    for p in range(Q):
         field[p] = (
             field[p]
             + halves(mxu(volume_rows[...], star_times(star_f, early_f, p, F)))
@@ -333,9 +344,10 @@
 
 def fourth_kernel(
     dofs, star, minus, plus, cluster, nb_all, codes, early, later, late, moved, scatter,
-    a, b, q_in, volume_rows, lift_rows, turn_rows, proj_rows,
-    out, own, face, flow, near,
+    a, b, q_in, volume_rows, lift_rows, turn_rows, proj_rows, outer,
+    out, kept, own, face, flow, near,
 ):
+    kept[...] = outer[...]
     kinds = cluster[...]
     fast = kinds == 0
     picks = scatter[...]
@@ -357,8 +369,7 @@
     )
     flux(plus, face, flow, E, True)
 
-    @pl.loop(0, Q)
-    def _(p):
+    for p in range(Q):
         out[p] = (
             out[p]
             + halves(mxu(volume_rows[...], star_times(star, own, p, E)))
@@ -379,38 +390,56 @@
         out[p] = jnp.where(active, value[0:35], dofs[p])
 
 
-def call(kernel, outs, args, scratch, scalars=0):
+def call(kernel, outs, args, scratch, scalars=0, copies=0, micros=5):
     vmem = pl.BlockSpec(memory_space=pltpu.VMEM)
     smem = pl.BlockSpec(memory_space=pltpu.SMEM)
+    place = pl.BlockSpec(memory_space=pl.ANY) if copies else vmem
+    if copies:
+        args = args[:scalars] + [
+            pltpu.with_memory_space_constraint(x, pltpu.HBM) for x in args[scalars:]
+        ]
     return pl.pallas_call(
         kernel,
         out_shape=[jax.ShapeDtypeStruct(*o) for o in outs],
-        in_specs=[smem] * scalars + [vmem] * (len(args) - scalars),
+        in_specs=[smem] * scalars + [place] * (len(args) - scalars),
         out_specs=[vmem] * len(outs),
-        scratch_shapes=[pltpu.VMEM(*s) for s in scratch],
+        scratch_shapes=[pltpu.VMEM(*s) for s in scratch]
+        + ([pltpu.SemaphoreType.DMA((copies,))] if copies else []),
         compiler_params=pltpu.CompilerParams(vmem_limit_bytes=48 * 1024 * 1024),
+        cost_estimate=pl.CostEstimate(
+            flops=int(micros * 1e9), bytes_accessed=1 << 20, transcendentals=0
+        ),
         name=kernel.__name__,
     )(*args)
 
 
-def exchange(inner, outer):
+def to_chips(inner, outer):
     count = lax.axis_size("dom")
     chips = count // 2
 
     def along(reach):
         def target(device):
             chip, core = device // 2, device % 2
-            return 2 * ((chip + (reach if core == 0 else -reach)) % chips) + core
+            to = chip + (reach if core == 0 else -reach)
+            return 2 * to + core if 0 <= to < chips else device ^ 1
 
         return [(device, target(device)) for device in range(count)]
 
-    pair = [(device, device ^ 1) for device in range(count)]
+    beside = to_pair(inner)
+    first = iota((1, LANES), 1) < 64
+    a = lax.ppermute(jnp.where(first, beside, outer), "dom", along(1))
+    b = lax.ppermute(jnp.where(first, outer, beside), "dom", along(2))
+    return a, b
+
+
+def to_pair(value):
+    count = lax.axis_size("dom")
+    return lax.ppermute(value, "dom", [(device, device ^ 1) for device in range(count)])
+
+
+def handed_on(outer, a, b):
     part = iota((1, LANES), 1) // 32
-    beside = lax.ppermute(inner, "dom", pair)
-    a = lax.ppermute(jnp.where(part < 2, beside, outer), "dom", along(1))
-    b = lax.ppermute(jnp.where(part < 2, outer, beside), "dom", along(2))
-    back = jnp.where(part == 0, outer, jnp.where(part == 3, b, a))
-    return a, b, lax.ppermute(back, "dom", pair)
+    return jnp.where(part == 0, outer, jnp.where(part == 3, b, a))
 
 
 def body(
@@ -429,34 +458,44 @@
 ):
     core = (lax.axis_index("dom") % 2).astype(jnp.int32).reshape(1)
     cluster = cluster.reshape(1, E)
+    star, flux_minus, flux_plus = (
+        jnp.transpose(x, (1, 2, 0, 3)) for x in (star, flux_minus, flux_plus)
+    )
     whole, compact, block = (Q, C, E), (Q, C, F), (Q * C, LANES)
     early, later, inner, outer = call(
         first_kernel,
         [(whole, F32), (whole, F32), (block, F32), (block, F32)],
         [core, dofs, star, stiffness, send_list],
-        [((2,) + whole, F32), ((C, 256), F32)],
+        [
+            ((2,) + whole, F32), ((C, 256), F32), ((Q, 35, E), F32), ((Q, Q, 3, E), F32),
+            ((3, 35, 35), F32), ((8, 32), jnp.int32),
+        ],
         1,
-    )
-    a, b, q_in = exchange(inner, outer)
+        20,
+    )
+    a, b = to_chips(inner, outer)
     (
-        field, star_f, plus_f, lines_f, scatter, nb_all, volume_rows, lift_rows, turn_rows, proj_rows
+        field, star_f, plus_f, lines_f, scatter, nb_all, volume_rows, lift_rows, turn_rows, proj_rows,
+        kept,
     ) = call(
         second_kernel,
         [
-            (compact, F32), ((3, Q, Q, F), F32), ((4, Q, Q, F), F32), ((8, F), jnp.int32),
+            (compact, F32), ((Q, Q, 3, F), F32), ((Q, Q, 4, F), F32), ((8, F), jnp.int32),
             ((F, E), BF16), ((4, E), jnp.int32),
             ((2 * C, 256), BF16), ((C, 192), BF16), ((192, 144), BF16), ((64, 144), BF16),
+            (block, F32),
         ],
         [
             core, dofs, star, flux_minus, flux_plus, cluster, neighbour, face_code, early,
-            stiffness, face_proj, face_lift, face_turn,
-        ],
-        [
-            ((4, Q, Q, F), F32), (compact, F32), ((Q, 64, F), F32), ((Q, 64, F), F32),
-            ((Q * C, F), F32), ((C, 256), F32), ((C, 192), F32), ((192, 144), F32),
+            stiffness, face_proj, face_lift, face_turn, outer,
+        ],
+        [
+            ((Q, Q, 4, F), F32), (compact, F32), ((Q, 64, F), F32), ((Q, 64, F), F32),
+            ((Q * C, 4 * F), F32), ((C, 256), F32), ((C, 192), F32), ((192, 144), F32),
         ],
         1,
     )
+    q_in = to_pair(handed_on(kept, a, b))
     moved, late, inner, outer = call(
         third_kernel,
         [(compact, F32), (whole, F32), (block, F32), (block, F32)],
@@ -466,25 +505,26 @@
         ],
         [
             ((2,) + compact, F32), ((2,) + compact, F32), ((Q, 64, F), F32), ((Q, 64, F), F32),
-            ((Q * C, F), F32), ((C, 256), F32),
+            ((Q * C, 4 * F), F32), ((C, 256), F32),
         ],
         1,
     )
-    a2, b2, q2 = exchange(inner, outer)
-    (partial,) = call(
+    a2, b2 = to_chips(inner, outer)
+    partial, kept = call(
         fourth_kernel,
-        [(whole, F32)],
+        [(whole, F32), (block, F32)],
         [
             dofs, star, flux_minus, flux_plus, cluster, nb_all, face_code, early, later, late, moved,
-            scatter, a, b, q_in, volume_rows, lift_rows, turn_rows, proj_rows,
-        ],
-        [(whole, F32), ((Q, 64, E), F32), ((Q, 64, E), F32), ((Q * C, E), F32)],
-    )
+            scatter, a, b, q_in, volume_rows, lift_rows, turn_rows, proj_rows, outer,
+        ],
+        [(whole, F32), ((Q, 64, E), F32), ((Q, 64, E), F32), ((Q * C, 4 * E), F32)],
+    )
+    q2 = to_pair(handed_on(kept, a2, b2))
     (out,) = call(
         fifth_kernel,
         [((Q, 35, E), F32)],
         [dofs, flux_plus, cluster, nb_all, face_code, partial, a2, b2, q2, lift_rows, turn_rows],
-        [((Q, 64, E), F32), ((Q, 64, E), F32), ((Q * C, E), F32)],
+        [((Q, 64, E), F32), ((Q, 64, E), F32), ((Q * C, 4 * E), F32)],
     )
     return out
 

time: 111 us -> 50.3 us (0.45)
  the two profiles are of different devices: /device:TPU:1 before, /device:TPU:25 now
where the time goes in v2:
time: 50.3 us; the launch traced here: 50.1 us
  Pallas kernels  28.5 us (57%)
  starting transfers between devices  15.6 us (31%)
  waiting for transfers between devices  4.08 us (8%)
  local copies, waits for them, and re-layouts  1.66 us (3%)
    pallas_call x5, Pallas kernels, call(): pl.pallas_call(kernel, out_shape=[jax.ShapeDtypeStruct(*o) for o in outs]...  28.5 us
    ppermute x2, starting transfers between devices, to_chips(): b = lax.ppermute(jnp.where(first, outer, beside), 'dom', along(2))  9.16 us
    ppermute x4, starting transfers between devices, to_pair(): lax.ppermute(value, 'dom', [(device, device ^ 1) for device in range(coun...  4.64 us
    ppermute x4, waiting for transfers between devices, to_pair(): lax.ppermute(value, 'dom', [(device, device ^ 1) for device in range(coun...  4.06 us
    ppermute x2, starting transfers between devices, to_chips(): a = lax.ppermute(jnp.where(first, beside, outer), 'dom', along(1))  1.76 us
    unnamed x30, local copies, waits for them, and re-layouts  1.66 us
  transfers between devices with their start and end apart: 8, of which 4 were waited for; matrix products, arithmetic and copies ran while one was open for 0% of the time, Pallas kernels for 25%

profile of v2, /device:TPU:25, one launch (start us, length us, event | category | flops | bytes accessed | tf_op | source)
XLA Modules:
  0.0 50.1 jit_solution(4791497347389977582)
XLA Ops:
  0.0 0.0 copy-start.13
  0.0 0.0 copy-start.12
  0.0 0.0 copy-start.1
  0.0 0.0 copy-start.2
  0.0 0.0 copy-start.3
  0.0 7.8 %first_kernel.1 = (f32[9,40,384]{2,1,0:T(8,128)S(1)}, f32[9,40,384]{2,1,0:T(8,128)S(1)}, f32[360,128]{1,0:T(8,128)S(1)}, f32[360,128]{1,0:T(8,128)S(1)}) custom-call(s32[1]{0:T(128)} %bitcast.1.core, f32[9,35,384]{2,1,0:T(8,128)} %dofs.7, f32[9,9,3,384]{3,2,1,0:T(4,128)} %bitcast.4, f32[3,35,35]{2,1,0:T(8,128)} %stiffness.3, s32[8,32]{1,0:T(8,128)} %send_list.1), custom_call_target="tpu_custom_call" | custom-call | flops 5000000000 | bytes 1048576 | tf_op jit(solution)/shard_map/first_kernel/pallas_call | solution.py:401
  7.8 0.0 copy-start.9
  7.9 0.8 %copy-done.9 = f32[9,40,384]{2,1,0:T(8,128)} copy-done((f32[9,40,384]{2,1,0:T(8,128)}, f32[9,40,384]{2,1,0:T(8,128)S(1)}, u32[]{:S(2)}) %copy-start.9) | copy-done | bytes 552984
  8.6 0.0 copy-start
  8.6 0.7 %collective-permute-start = (f32[360,128]{1,0:T(8,128)S(1)}, f32[360,128]{1,0:T(8,128)S(1)}, u32[]{:S(2)}, u32[]{:S(2)}) collective-permute-start(f32[360,128]{1,0:T(8,128)S(1)} %get-tuple-element.30), channel_id=1, source_target_pairs={{0,1},{1,0},{2,3},{3,2},{4,5},{5,4},{6,7},{7,6},{8,9},{9,8},{10,11... | collective-permute-start | bytes 552968 | tf_op jit(solution)/shard_map/ppermute | solution.py:437
  9.3 0.0 copy-done.13
  9.3 0.0 copy-done.11
  9.3 0.0 copy-done.12
  9.4 0.1 copy.14.lift
  9.5 0.9 %collective-permute-done = f32[360,128]{1,0:T(8,128)S(1)} collective-permute-done((f32[360,128]{1,0:T(8,128)S(1)}, f32[360,128]{1,0:T(8,128)S(1)}, u32[]{:S(2)}, u32[]{:S(2)}) %collective-permute-start) | collective-permute-done | bytes 184352 | tf_op jit(solution)/shard_map/ppermute | solution.py:437
  10.4 0.0 copy-start.4
  10.4 0.0 copy-start.5
  10.4 0.0 copy-start.7
  10.4 0.0 copy-start.6
  10.4 6.5 %collective-permute-start.2 = (f32[360,128]{1,0:T(8,128)S(1)}, f32[360,128]{1,0:T(8,128)S(1)}, u32[]{:S(2)}, u32[]{:S(2)}) collective-permute-start(f32[360,128]{1,0:T(8,128)S(1)} %get-tuple-element.49), channel_id=1, source_target_pairs={{0,4},{1,0},{2,6},{3,2},{4,8},{5,1},{6,10},{7,3},{8,12},{9,5},{10,... | collective-permute-start | bytes 552968 | tf_op jit(solution)/shard_map/ppermute | solution.py:431
  16.9 0.9 %collective-permute-start.1 = (f32[360,128]{1,0:T(8,128)S(1)}, f32[360,128]{1,0:T(8,128)S(1)}, u32[]{:S(2)}, u32[]{:S(2)}) collective-permute-start(f32[360,128]{1,0:T(8,128)S(1)} %get-tuple-element.50), channel_id=1, source_target_pairs={{0,2},{1,0},{2,4},{3,1},{4,6},{5,3},{6,8},{7,5},{8,10},{9,7},{10,1... | collective-permute-start | bytes 552968 | tf_op jit(solution)/shard_map/ppermute | solution.py:430
  17.8 0.0 copy-done.1
  17.8 0.0 copy-done.2
  17.8 0.0 copy-done.3
  17.8 0.0 copy-done
  17.8 0.0 copy-done.4
  17.8 0.0 copy-done.5
  17.8 0.0 copy-done.7
  17.8 0.0 copy-done.6
  17.8 4.8 %second_kernel.1 = (f32[9,40,128]{2,1,0:T(8,128)S(1)}, f32[9,9,3,128]{3,2,1,0:T(4,128)S(1)}, f32[9,9,4,128]{3,2,1,0:T(4,128)S(1)}, s32[8,128]{1,0:T(8,128)S(1)},...) custom-call(s32[1]{0:T(128)} %bitcast.1.core, ...), custom_call_target="tpu_custom_call" | custom-call | flops 5000000000 | bytes 1048576 | tf_op jit(solution)/shard_map/second_kernel/pallas_call | solution.py:401
  22.7 0.0 copy-start.10
  22.7 0.0 collective-permute-done.2.b
  22.7 0.0 collective-permute-done.1.a
  22.7 2.2 %collective-permute-start.3 = (f32[360,128]{1,0:T(8,128)S(1)}, f32[360,128]{1,0:T(8,128)S(1)}, u32[]{:S(2)}, u32[]{:S(2)}) collective-permute-start(f32[360,128]{1,0:T(8,128)S(1)} %select_select_fusion.1), channel_id=1, source_target_pairs={{0,1},{1,0},{2,3},{3,2},{4,5},{5,4},{6,7},{7,6},{8,9},{9,8},{10,11... | collective-permute-start | bytes 552968 | tf_op jit(solution)/shard_map/ppermute | solution.py:437
  25.0 1.1 %collective-permute-done.3.q_in = f32[360,128]{1,0:T(8,128)S(1)} collective-permute-done((f32[360,128]{1,0:T(8,128)S(1)}, f32[360,128]{1,0:T(8,128)S(1)}, u32[]{:S(2)}, u32[]{:S(2)}) %collective-permute-start.3) | collective-permute-done | bytes 184352 | tf_op jit(solution)/shard_map/ppermute | solution.py:437
  26.1 0.0 copy-done.10
  26.1 0.7 %copy-done.8 = s32[8,32]{1,0:T(8,128)S(1)} copy-done((s32[8,32]{1,0:T(8,128)S(1)}, s32[8,32]{1,0:T(8,128)}, u32[]{:S(2)}) %copy-start.8) | copy-done | bytes 1048
  26.7 4.2 %third_kernel.1 = (f32[9,40,128]{2,1,0:T(8,128)S(1)}, f32[9,40,384]{2,1,0:T(8,128)S(1)}, f32[360,128]{1,0:T(8,128)S(1)}, f32[360,128]{1,0:T(8,128)S(1)}) custom-call(s32[1]{0:T(128)} %bitcast.1.core, f32[3,35,35]{2,1,0:T(8,128)S(1)} %copy-done.4, s32[8,32]{1,0:T(8,128)S(1)} %copy-done.8, f32[360,128]{1,0:T(8,128)S(1)} %collective-permute-done.1.a, ...), custom_call_target="tpu_custom_call" | custom-call | flops 5000000000 | bytes 1048576 | tf_op jit(solution)/shard_map/third_kernel/pallas_call | solution.py:401
  31.0 0.5 collective-permute-start.4
  31.4 1.1 %collective-permute-done.4 = f32[360,128]{1,0:T(8,128)S(1)} collective-permute-done((f32[360,128]{1,0:T(8,128)S(1)}, f32[360,128]{1,0:T(8,128)S(1)}, u32[]{:S(2)}, u32[]{:S(2)}) %collective-permute-start.4) | collective-permute-done | bytes 184352 | tf_op jit(solution)/shard_map/ppermute | solution.py:437
  32.5 2.7 %collective-permute-start.6 = (f32[360,128]{1,0:T(8,128)S(1)}, f32[360,128]{1,0:T(8,128)S(1)}, u32[]{:S(2)}, u32[]{:S(2)}) collective-permute-start(f32[360,128]{1,0:T(8,128)S(1)} %get-tuple-element.47), channel_id=1, source_target_pairs={{0,4},{1,0},{2,6},{3,2},{4,8},{5,1},{6,10},{7,3},{8,12},{9,5},{10,... | collective-permute-start | bytes 552968 | tf_op jit(solution)/shard_map/ppermute | solution.py:431
  35.2 0.9 %collective-permute-start.5 = (f32[360,128]{1,0:T(8,128)S(1)}, f32[360,128]{1,0:T(8,128)S(1)}, u32[]{:S(2)}, u32[]{:S(2)}) collective-permute-start(f32[360,128]{1,0:T(8,128)S(1)} %get-tuple-element.48), channel_id=1, source_target_pairs={{0,2},{1,0},{2,4},{3,1},{4,6},{5,3},{6,8},{7,5},{8,10},{9,7},{10,1... | collective-permute-start | bytes 552968 | tf_op jit(solution)/shard_map/ppermute | solution.py:430
  36.1 7.7 %fourth_kernel.1 = (f32[9,40,384]{2,1,0:T(8,128)S(1)}, f32[360,128]{1,0:T(8,128)S(1)}) custom-call(f32[9,35,384]{2,1,0:T(8,128)S(1)} %copy-done, f32[9,9,3,384]{3,2,1,0:T(4,128)S(1)} %bitcast.6, f32[9,9,4,384]{3,2,1,0:T(4,128)S(1)} %bitcast.8, f32[9,9,4,384]{3,2,1,0:T(4,128)S(1)} %bitcast.10, s32[1,384]{1,0:T(1,128)S(1)} %reshape.53.cluster, ...), custom_call_target="tpu_custom_call" | custom-call | flops 5000000000 | bytes 1048576 | tf_op jit(solution)/shard_map/fourth_kernel/pallas_call | solution.py:401
  43.8 0.0 collective-permute-done.6.b
  43.8 0.0 collective-permute-done.5.a
  43.8 1.3 %collective-permute-start.7 = (f32[360,128]{1,0:T(8,128)S(1)}, f32[360,128]{1,0:T(8,128)S(1)}, u32[]{:S(2)}, u32[]{:S(2)}) collective-permute-start(f32[360,128]{1,0:T(8,128)S(1)} %select_select_fusion), channel_id=1, source_target_pairs={{0,1},{1,0},{2,3},{3,2},{4,5},{5,4},{6,7},{7,6},{8,9},{9,8},{10,11... | collective-permute-start | bytes 552968 | tf_op jit(solution)/shard_map/ppermute | solution.py:437
  45.1 1.1 %collective-permute-done.7.q_in = f32[360,128]{1,0:T(8,128)S(1)} collective-permute-done((f32[360,128]{1,0:T(8,128)S(1)}, f32[360,128]{1,0:T(8,128)S(1)}, u32[]{:S(2)}, u32[]{:S(2)}) %collective-permute-start.7) | collective-permute-done | bytes 184352 | tf_op jit(solution)/shard_map/ppermute | solution.py:437
  46.1 4.0 %fifth_kernel.1 = f32[9,35,384]{2,1,0:T(8,128)} custom-call(f32[9,35,384]{2,1,0:T(8,128)S(1)} %copy-done, f32[9,9,4,384]{3,2,1,0:T(4,128)S(1)} %bitcast.11, s32[1,384]{1,0:T(1,128)S(1)} %reshape.53.cluster, s32[4,384]{1,0:T(4,128)S(1)} %get-tuple-element.28.nb_all, s32[4,384]{1,0:T(4,128)S(1)} %copy-done.7, f32[9,40,384]{2,1,0:T(8,128)S(1)} %get-tuple-element.44.partial, ...), custom_call_target="tpu_custom_call" | custom-call | flops 5000000000 | bytes 1048576 | tf_op jit(solution)/shard_map/fifth_kernel/pallas_call | solution.py:401
  (10 shorter events, 0.2 us)
Async XLA Ops:
  0.0 9.3 %copy-start.13 = (s32[384]{0:T(512)S(1)}, s32[384]{0:T(512)}, u32[]{:S(2)}) copy-start(s32[384]{0:T(512)} %param.16) | copy-start | bytes 4612
  0.0 9.3 %copy-start.11 = (f32[4,15,35]{2,0,1:T(4,128)S(1)}, f32[4,15,35]{2,0,1:T(4,128)}, u32[]{:S(2)}) copy-start(f32[4,15,35]{2,0,1:T(4,128)} %param.21) | copy-start | bytes 25204
  0.0 9.3 %copy-start.12 = (f32[4,35,15]{1,0,2:T(4,128)S(1)}, f32[4,35,15]{1,0,2:T(4,128)}, u32[]{:S(2)}) copy-start(f32[4,35,15]{1,0,2:T(4,128)} %param.22) | copy-start | bytes 25204
  0.0 17.8 %copy-start.1 = (f32[3,9,9,384]{3,0,2,1:T(4,128)S(1)}, f32[3,9,9,384]{3,0,2,1:T(4,128)}, u32[]{:S(2)}) copy-start(f32[3,9,9,384]{3,0,2,1:T(4,128)} %param.13) | copy-start | bytes 1119748
  0.0 17.8 %copy-start.2 = (f32[4,9,9,384]{3,0,2,1:T(4,128)S(1)}, f32[4,9,9,384]{3,0,2,1:T(4,128)}, u32[]{:S(2)}) copy-start(f32[4,9,9,384]{3,0,2,1:T(4,128)} %param.14) | copy-start | bytes 1492996
  0.0 17.7 %copy-start.3 = (f32[4,9,9,384]{3,0,2,1:T(4,128)S(1)}, f32[4,9,9,384]{3,0,2,1:T(4,128)}, u32[]{:S(2)}) copy-start(f32[4,9,9,384]{3,0,2,1:T(4,128)} %param.15) | copy-start | bytes 1492996
  7.8 0.8 %copy-start.9 = (f32[9,40,384]{2,1,0:T(8,128)}, f32[9,40,384]{2,1,0:T(8,128)S(1)}, u32[]{:S(2)}) copy-start(f32[9,40,384]{2,1,0:T(8,128)S(1)} %get-tuple-element.29.later) | copy-start | bytes 1658884
  8.6 9.1 %copy-start = (f32[9,35,384]{2,1,0:T(8,128)S(1)}, f32[9,35,384]{2,1,0:T(8,128)}, u32[]{:S(2)}) copy-start(f32[9,35,384]{2,1,0:T(8,128)} %dofs.7) | copy-start | bytes 1451524
  8.6 1.7 %collective-permute-start = (f32[360,128]{1,0:T(8,128)S(1)}, f32[360,128]{1,0:T(8,128)S(1)}, u32[]{:S(2)}, u32[]{:S(2)}) collective-permute-start(f32[360,128]{1,0:T(8,128)S(1)} %get-tuple-element.30), channel_id=1, source_target_pairs={{0,1},{1,0},{2,3},{3,2},{4,5},{5,4},{6,7},{7,6},{8,9},{9,8},{10,11... | collective-permute-start | bytes 552968 | tf_op jit(solution)/shard_map/ppermute | solution.py:437
  10.4 7.4 %copy-start.4 = (f32[3,35,35]{2,1,0:T(8,128)S(1)}, f32[3,35,35]{2,1,0:T(8,128)}, u32[]{:S(2)}) copy-start(f32[3,35,35]{2,1,0:T(8,128)} %stiffness.3) | copy-start | bytes 44104
  10.4 7.4 %copy-start.5 = (f32[3,15,15]{2,1,0:T(8,128)S(1)}, f32[3,15,15]{2,1,0:T(8,128)}, u32[]{:S(2)}) copy-start(f32[3,15,15]{2,1,0:T(8,128)} %turn.1) | copy-start | bytes 8104
  10.4 7.4 %copy-start.7 = (s32[4,384]{1,0:T(4,128)S(1)}, s32[4,384]{1,0:T(4,128)}, u32[]{:S(2)}) copy-start(s32[4,384]{1,0:T(4,128)} %codes.5) | copy-start | bytes 18436
  10.4 7.4 %copy-start.6 = (s32[4,384]{1,0:T(4,128)S(1)}, s32[4,384]{1,0:T(4,128)}, u32[]{:S(2)}) copy-start(s32[4,384]{1,0:T(4,128)} %neighbour.1) | copy-start | bytes 18436
  10.4 12.2 %collective-permute-start.2 = (f32[360,128]{1,0:T(8,128)S(1)}, f32[360,128]{1,0:T(8,128)S(1)}, u32[]{:S(2)}, u32[]{:S(2)}) collective-permute-start(f32[360,128]{1,0:T(8,128)S(1)} %get-tuple-element.49), channel_id=1, source_target_pairs={{0,4},{1,0},{2,6},{3,2},{4,8},{5,1},{6,10},{7,3},{8,12},{9,5},{10,... | collective-permute-start | bytes 552968 | tf_op jit(solution)/shard_map/ppermute | solution.py:431
  16.9 5.8 %collective-permute-start.1 = (f32[360,128]{1,0:T(8,128)S(1)}, f32[360,128]{1,0:T(8,128)S(1)}, u32[]{:S(2)}, u32[]{:S(2)}) collective-permute-start(f32[360,128]{1,0:T(8,128)S(1)} %get-tuple-element.50), channel_id=1, source_target_pairs={{0,2},{1,0},{2,4},{3,1},{4,6},{5,3},{6,8},{7,5},{8,10},{9,7},{10,1... | collective-permute-start | bytes 552968 | tf_op jit(solution)/shard_map/ppermute | solution.py:430
  22.7 3.4 %copy-start.10 = (f32[9,40,384]{2,1,0:T(8,128)S(1)}, f32[9,40,384]{2,1,0:T(8,128)}, u32[]{:S(2)}) copy-start(f32[9,40,384]{2,1,0:T(8,128)} %copy-done.9) | copy-start | bytes 1658884
  22.7 3.3 %collective-permute-start.3 = (f32[360,128]{1,0:T(8,128)S(1)}, f32[360,128]{1,0:T(8,128)S(1)}, u32[]{:S(2)}, u32[]{:S(2)}) collective-permute-start(f32[360,128]{1,0:T(8,128)S(1)} %select_select_fusion.1), channel_id=1, source_target_pairs={{0,1},{1,0},{2,3},{3,2},{4,5},{5,4},{6,7},{7,6},{8,9},{9,8},{10,11... | collective-permute-start | bytes 552968 | tf_op jit(solution)/shard_map/ppermute | solution.py:437
  26.1 0.7 %copy-start.8 = (s32[8,32]{1,0:T(8,128)S(1)}, s32[8,32]{1,0:T(8,128)}, u32[]{:S(2)}) copy-start(s32[8,32]{1,0:T(8,128)} %send_list.1) | copy-start | bytes 3076
  31.0 1.5 %collective-permute-start.4 = (f32[360,128]{1,0:T(8,128)S(1)}, f32[360,128]{1,0:T(8,128)S(1)}, u32[]{:S(2)}, u32[]{:S(2)}) collective-permute-start(f32[360,128]{1,0:T(8,128)S(1)} %get-tuple-element.45), channel_id=1, source_target_pairs={{0,1},{1,0},{2,3},{3,2},{4,5},{5,4},{6,7},{7,6},{8,9},{9,8},{10,11... | collective-permute-start | bytes 552968 | tf_op jit(solution)/shard_map/ppermute | solution.py:437
  32.5 11.3 %collective-permute-start.6 = (f32[360,128]{1,0:T(8,128)S(1)}, f32[360,128]{1,0:T(8,128)S(1)}, u32[]{:S(2)}, u32[]{:S(2)}) collective-permute-start(f32[360,128]{1,0:T(8,128)S(1)} %get-tuple-element.47), channel_id=1, source_target_pairs={{0,4},{1,0},{2,6},{3,2},{4,8},{5,1},{6,10},{7,3},{8,12},{9,5},{10,... | collective-permute-start | bytes 552968 | tf_op jit(solution)/shard_map/ppermute | solution.py:431
  35.2 8.6 %collective-permute-start.5 = (f32[360,128]{1,0:T(8,128)S(1)}, f32[360,128]{1,0:T(8,128)S(1)}, u32[]{:S(2)}, u32[]{:S(2)}) collective-permute-start(f32[360,128]{1,0:T(8,128)S(1)} %get-tuple-element.48), channel_id=1, source_target_pairs={{0,2},{1,0},{2,4},{3,1},{4,6},{5,3},{6,8},{7,5},{8,10},{9,7},{10,1... | collective-permute-start | bytes 552968 | tf_op jit(solution)/shard_map/ppermute | solution.py:430
  43.8 2.3 %collective-permute-start.7 = (f32[360,128]{1,0:T(8,128)S(1)}, f32[360,128]{1,0:T(8,128)S(1)}, u32[]{:S(2)}, u32[]{:S(2)}) collective-permute-start(f32[360,128]{1,0:T(8,128)S(1)} %select_select_fusion), channel_id=1, source_target_pairs={{0,1},{1,0},{2,3},{3,2},{4,5},{5,4},{6,7},{7,6},{8,9},{9,8},{10,11... | collective-permute-start | bytes 552968 | tf_op jit(solution)/shard_map/ppermute | solution.py:437

commit v3 on v2

--- a/solution.py
+++ b/solution.py
@@ -48,6 +48,11 @@
     )
     mode = lax.GatherScatterMode.PROMISE_IN_BOUNDS
     return lax.gather(x, at[..., None], numbers, (1, 1), mode=mode)
+
+
+def both(x, right):
+    high, low = split(x)
+    return mxu(high, right) + mxu(low, right)
 
 
 def lanes_of(width):
@@ -135,8 +140,7 @@
     return jnp.concatenate([rows[i : i + 1, :] for i in range(4)], axis=1)
 
 
-def near_faces(parts, neighbour, codes, turn_rows, near_ref, face_ref, width):
-    total = None
+def gathered(parts, neighbour, width, total=None):
     wanted = beside(neighbour)
     for arrays, first, mask in parts:
         columns = arrays[0].shape[1]
@@ -147,7 +151,10 @@
         for array in arrays:
             piece = mxu(array, pick)
             total = piece if total is None else total + piece
-    near_ref[...] = total
+    return total
+
+
+def near_faces(near_ref, codes, turn_rows, face_ref, width):
     code = beside(codes)
     for q in range(Q):
         every = mxu(turn_rows, three_parts(padded48(near_ref[q * C : (q + 1) * C, :])))
@@ -164,7 +171,7 @@
 
 def first_kernel(
     core, dofs_in, star_in, stiffness_in, send_list_in,
-    early, later, inner, outer,
+    early, later, inner, outer, rows, pick,
     cur, pad, dofs, star, stiffness, send_list, done,
 ):
     small = [
@@ -179,7 +186,8 @@
         cur[0, q, 32:C, :] = jnp.zeros((8, E), F32)
     small[0].wait()
     small[1].wait()
-    rows = stiffness_rows(stiffness, False, -1.0, pad)
+    rows[...] = stiffness_rows(stiffness, False, -1.0, pad)
+    pick[...] = send_pick(core, send_list)
     for q in range(Q):
         fields[q].wait()
         cur[0, q, 0:35, :] = dofs[q]
@@ -193,10 +201,8 @@
 
     for copy in stars:
         copy.wait()
-    taylor(star, rows, cur, E, add)
-    pick = send_pick(core, send_list)
-    high, low = split(flat(early[...]))
-    sent = mxu(high, pick) + mxu(low, pick)
+    taylor(star, rows[...], cur, E, add)
+    sent = both(flat(early[...]), pick[...])
     inner[...] = sent[:, :LANES]
     outer[...] = sent[:, LANES:]
 
@@ -229,9 +235,10 @@
 
 
 def second_kernel(
-    core, dofs, star, minus, plus, cluster, neighbour, codes, early,
+    core, dofs, star, minus, plus, cluster, neighbour, codes, early, later, pick,
     stiffness, proj, lift, turn, outer,
     field, star_f, plus_f, lines_f, scatter, nb_all, volume_rows, lift_rows, turn_rows, proj_rows, kept,
+    near_medium, steady, route,
     minus_f, early_f, face, flow, near, pad, pad_lift, pad_turn,
 ):
     kept[...] = outer[...]
@@ -240,15 +247,15 @@
     total = jnp.zeros((35, 192), F32)
     for i in range(4):
         place = (iota((15, 192), 1) % 64 == i * G + iota((15, 192), 0)).astype(F32)
-        total = total - exact(lift[i], place)
+        total = total - exact(lift[:, i, :], place, (((0,), (0,)), ((), ())))
     pad_lift[0:35, :] = total
     lift_rows[...] = three(pad_lift[...], 128)
     place = (iota((35, 144), 1) % 48 == iota((35, 144), 0)).astype(F32)
     pad_turn[...] = jnp.zeros((192, 144), F32)
     for i in range(4):
-        pad_turn[i * G : i * G + 15, :] = exact(proj[i], place)
+        pad_turn[i * G : i * G + 15, :] = exact(proj[:, i, :], place)
     proj_rows[...] = three(pad_turn[0:64, :], 96)
-    projs = [exact(proj[i], place) for i in range(4)]
+    projs = [exact(proj[:, i, :], place) for i in range(4)]
     for i in range(4):
         for h in range(3):
             at = (3 * i + h) * G
@@ -291,8 +298,13 @@
 
     own_faces(early_f, proj_rows[...], face, F)
     flux(minus_f, face, flow, F, False)
-    near_faces([(split(flat(early[...])), 0, None)], nb, code, turn_rows[...], near, face, F)
+    parts = split(flat(early[...]))
+    near[...] = gathered([(parts, 0, None)], nb, F)
+    near_faces(near, code, turn_rows[...], face, F)
     flux(plus_f, face, flow, F, True)
+    near_medium[...] = gathered([(parts, 0, kinds == 1)], table, E)
+    steady[...] = both(jnp.where(kinds == 0, 0.0, flat(later[...])), pick[...])
+    route[...] = mxu(picks, pick[...]).astype(BF16)
 
     for p in range(Q):
         field[p] = (
@@ -303,37 +315,38 @@
 
 
 def third_kernel(
-    core, stiffness, send_list, a, b, q_in, field, star_f, plus_f, lines_f, scatter, cluster, later, dofs,
-    lift_rows, turn_rows,
-    moved, late, inner, outer,
-    late_f, cur, face, flow, near, pad,
+    rows, a, b, q_in, field, star_f, plus_f, lines_f, steady, route, lift_rows, turn_rows,
+    moved_f, late_f, inner, outer,
+    cur, face, flow, near,
 ):
-    ghosts = ghost_array(a, b, q_in)
-    near_faces([(split(ghosts), E, None)], lines_f[0:4, :], lines_f[4:8, :], turn_rows[...], near, face, F)
+    ghosts = split(ghost_array(a, b, q_in))
+    near[...] = gathered([(ghosts, E, None)], lines_f[0:4, :], F)
+    near_faces(near, lines_f[4:8, :], turn_rows[...], face, F)
     flux(plus_f, face, flow, F, False)
     for p in range(Q):
         value = field[p] + mxu(lift_rows[...], three_parts(flow[p]))
         cur[0, p] = value
-        late_f[0, p] = value
-        late_f[1, p] = value
-    rows = stiffness_rows(stiffness, False, -1.0, pad)
+        moved_f[p] = value
+        late_f[p] = value
 
     def add(level, p, value):
-        late_f[0, p] = late_f[0, p] + value * (1.0 / math.factorial(level + 2))
-
-    taylor(star_f, rows, cur, F, add)
-    fast = cluster[...] == 0
-    picks = scatter[...]
-    for p in range(Q):
-        high, low = split(late_f[0, p])
-        late[p] = jnp.where(fast, mxu(high, picks) + mxu(low, picks), later[p])
-    pick = send_pick(core, send_list)
-    high, low = split(flat(late[...]))
-    sent = mxu(high, pick) + mxu(low, pick)
+        late_f[p] = late_f[p] + value * (1.0 / math.factorial(level + 2))
+
+    taylor(star_f, rows[...], cur, F, add)
+    sent = steady[...] + both(flat(late_f[...]), route[...])
     inner[...] = sent[:, :LANES]
     outer[...] = sent[:, LANES:]
+
+
+def spread_kernel(moved_f, late_f, scatter, cluster, later, dofs, start, late):
+    fast = cluster[...] == 0
+    moved = both(flat(moved_f[...]), scatter[...])
+    fresh = both(flat(late_f[...]), scatter[...])
     for p in range(Q):
-        moved[p] = late_f[1, p]
+        rows = slice(p * C, (p + 1) * C)
+        late[p] = jnp.where(fast, fresh[rows], later[p])
+        start[p] = moved[rows]
+        start[p, 0:35, :] = jnp.where(fast, start[p, 0:35, :], dofs[p])
 
 
 def ghost_array(a, b, q_in):
@@ -343,35 +356,27 @@
 
 
 def fourth_kernel(
-    dofs, star, minus, plus, cluster, nb_all, codes, early, later, late, moved, scatter,
+    start, star, minus, plus, cluster, nb_all, codes, early, late, near_medium,
     a, b, q_in, volume_rows, lift_rows, turn_rows, proj_rows, outer,
-    out, kept, own, face, flow, near,
+    out, kept,
+    own, face, flow, near,
 ):
     kept[...] = outer[...]
     kinds = cluster[...]
-    fast = kinds == 0
-    picks = scatter[...]
     for p in range(Q):
-        own[p] = jnp.where(fast, late[p], early[p] + later[p])
-        high, low = split(moved[p])
-        out[p] = jnp.where(fast, mxu(high, picks) + mxu(low, picks), 0.0)
-        out[p, 0:35, :] = jnp.where(fast, out[p, 0:35, :], dofs[p])
+        own[p] = jnp.where(kinds == 0, late[p], early[p] + late[p])
     own_faces(own, proj_rows[...], face, E)
     flux(minus, face, flow, E, False)
-    ghosts = ghost_array(a, b, q_in)
-    near_faces(
-        [
-            (split(flat(late[...])), 0, None),
-            (split(flat(early[...])), 0, kinds == 1),
-            (split(ghosts), E, kinds == 1),
-        ],
-        nb_all[...], codes[...], turn_rows[...], near, face, E,
-    )
+    parts = [
+        (split(flat(late[...])), 0, None),
+        (split(ghost_array(a, b, q_in)), E, kinds == 1),
+    ]
+    near[...] = gathered(parts, nb_all[...], E, near_medium[...])
+    near_faces(near, codes[...], turn_rows[...], face, E)
     flux(plus, face, flow, E, True)
-
     for p in range(Q):
         out[p] = (
-            out[p]
+            start[p]
             + halves(mxu(volume_rows[...], star_times(star, own, p, E)))
             + mxu(lift_rows[...], three_parts(flow[p]))
         )
@@ -381,8 +386,9 @@
     dofs, plus, cluster, nb_all, codes, partial, a, b, q_in, lift_rows, turn_rows,
     out, face, flow, near,
 ):
-    ghosts = ghost_array(a, b, q_in)
-    near_faces([(split(ghosts), E, None)], nb_all[...], codes[...], turn_rows[...], near, face, E)
+    ghosts = split(ghost_array(a, b, q_in))
+    near[...] = gathered([(ghosts, E, None)], nb_all[...], E)
+    near_faces(near, codes[...], turn_rows[...], face, E)
     flux(plus, face, flow, E, False)
     active = cluster[...] < 2
     for p in range(Q):
@@ -405,7 +411,7 @@
         out_specs=[vmem] * len(outs),
         scratch_shapes=[pltpu.VMEM(*s) for s in scratch]
         + ([pltpu.SemaphoreType.DMA((copies,))] if copies else []),
-        compiler_params=pltpu.CompilerParams(vmem_limit_bytes=48 * 1024 * 1024),
+        compiler_params=pltpu.CompilerParams(vmem_limit_bytes=10 * 1024 * 1024),
         cost_estimate=pl.CostEstimate(
             flops=int(micros * 1e9), bytes_accessed=1 << 20, transcendentals=0
         ),
@@ -461,10 +467,14 @@
     star, flux_minus, flux_plus = (
         jnp.transpose(x, (1, 2, 0, 3)) for x in (star, flux_minus, flux_plus)
     )
+    face_proj, face_lift = jnp.transpose(face_proj, (1, 0, 2)), jnp.transpose(face_lift, (2, 0, 1))
     whole, compact, block = (Q, C, E), (Q, C, F), (Q * C, LANES)
-    early, later, inner, outer = call(
+    early, later, inner, outer, rows, pick = call(
         first_kernel,
-        [(whole, F32), (whole, F32), (block, F32), (block, F32)],
+        [
+            (whole, F32), (whole, F32), (block, F32), (block, F32),
+            ((2 * C, 256), BF16), ((E, GHOST), BF16),
+        ],
         [core, dofs, star, stiffness, send_list],
         [
             ((2,) + whole, F32), ((C, 256), F32), ((Q, 35, E), F32), ((Q, Q, 3, E), F32),
@@ -476,17 +486,17 @@
     a, b = to_chips(inner, outer)
     (
         field, star_f, plus_f, lines_f, scatter, nb_all, volume_rows, lift_rows, turn_rows, proj_rows,
-        kept,
+        kept, near_medium, steady, route,
     ) = call(
         second_kernel,
         [
             (compact, F32), ((Q, Q, 3, F), F32), ((Q, Q, 4, F), F32), ((8, F), jnp.int32),
             ((F, E), BF16), ((4, E), jnp.int32),
             ((2 * C, 256), BF16), ((C, 192), BF16), ((192, 144), BF16), ((64, 144), BF16),
-            (block, F32),
-        ],
-        [
-            core, dofs, star, flux_minus, flux_plus, cluster, neighbour, face_code, early,
+            (block, F32), ((Q * C, 4 * E), F32), ((Q * C, GHOST), F32), ((F, GHOST), BF16),
+        ],
+        [
+            core, dofs, star, flux_minus, flux_plus, cluster, neighbour, face_code, early, later, pick,
             stiffness, face_proj, face_lift, face_turn, outer,
         ],
         [
@@ -496,26 +506,30 @@
         1,
     )
     q_in = to_pair(handed_on(kept, a, b))
-    moved, late, inner, outer = call(
+    moved_f, late_f, inner, outer = call(
         third_kernel,
-        [(compact, F32), (whole, F32), (block, F32), (block, F32)],
-        [
-            core, stiffness, send_list, a, b, q_in, field, star_f, plus_f, lines_f, scatter, cluster,
-            later, dofs, lift_rows, turn_rows,
-        ],
-        [
-            ((2,) + compact, F32), ((2,) + compact, F32), ((Q, 64, F), F32), ((Q, 64, F), F32),
-            ((Q * C, 4 * F), F32), ((C, 256), F32),
-        ],
-        1,
+        [(compact, F32), (compact, F32), (block, F32), (block, F32)],
+        [
+            rows, a, b, q_in, field, star_f, plus_f, lines_f, steady, route, lift_rows, turn_rows
+        ],
+        [
+            ((2,) + compact, F32), ((Q, 64, F), F32), ((Q, 64, F), F32), ((Q * C, 4 * F), F32),
+        ],
     )
     a2, b2 = to_chips(inner, outer)
+    start, late = call(
+        spread_kernel,
+        [(whole, F32), (whole, F32)],
+        [moved_f, late_f, scatter, cluster, later, dofs],
+        [],
+        micros=1,
+    )
     partial, kept = call(
         fourth_kernel,
         [(whole, F32), (block, F32)],
         [
-            dofs, star, flux_minus, flux_plus, cluster, nb_all, face_code, early, later, late, moved,
-            scatter, a, b, q_in, volume_rows, lift_rows, turn_rows, proj_rows, outer,
+            start, star, flux_minus, flux_plus, cluster, nb_all, face_code, early, late, near_medium,
+            a, b, q_in, volume_rows, lift_rows, turn_rows, proj_rows, outer,
         ],
         [(whole, F32), ((Q, 64, E), F32), ((Q, 64, E), F32), ((Q * C, 4 * E), F32)],
     )

time: 50.3 us -> 48.3 us (0.960)
  local copies, waits for them, and re-layouts: 1.66 us -> 0.05 us
    unnamed x30 -> x22, local copies, waits for them, and re-layouts: 1.66 us -> 0.04 us
    pallas_call x5 -> x6, Pallas kernels: 28.5 us -> 28.3 us  [call(): pl.pallas_call(kernel, out_shape=[jax.ShapeDtypeStruct(*o) for o in outs]...]
  transfers between devices with their start and end apart: 8 -> 8, of which waited for: 4 -> 4; matrix products, arithmetic and copies ran while one was open for 0% -> 0% of each run, Pallas kernels for 25% -> 27%
where the time goes in v3:
time: 48.3 us; the launch traced here: 48.2 us
  Pallas kernels  28.3 us (59%)
  starting transfers between devices  15.8 us (33%)
  waiting for transfers between devices  3.67 us (8%)
    pallas_call x6, Pallas kernels, call(): pl.pallas_call(kernel, out_shape=[jax.ShapeDtypeStruct(*o) for o in outs]...  28.3 us
    ppermute x2, starting transfers between devices, to_chips(): b = lax.ppermute(jnp.where(first, outer, beside), 'dom', along(2))  9.16 us
    ppermute x4, starting transfers between devices, to_pair(): lax.ppermute(value, 'dom', [(device, device ^ 1) for device in range(coun...  4.91 us
    ppermute x4, waiting for transfers between devices, to_pair(): lax.ppermute(value, 'dom', [(device, device ^ 1) for device in range(coun...  3.66 us
    ppermute x2, starting transfers between devices, to_chips(): a = lax.ppermute(jnp.where(first, beside, outer), 'dom', along(1))  1.76 us
  transfers between devices with their start and end apart: 8, of which 4 were waited for; matrix products, arithmetic and copies ran while one was open for 0% of the time, Pallas kernels for 27%

profile of v3, /device:TPU:25, one launch (start us, length us, event | category | flops | bytes accessed | tf_op | source)
XLA Modules:
  0.0 48.2 jit_solution(11065513961439666914)
XLA Ops:
  0.0 0.0 copy-start.10
  0.0 0.0 copy-start
  0.0 0.0 copy-start.1
  0.0 0.0 copy-start.2
  0.0 0.0 copy-start.3
  0.0 0.0 copy-start.4
  0.0 0.0 copy-start.5
  0.0 0.0 copy-start.6
  0.1 0.0 copy-start.7
  0.1 0.0 copy-start.8
  0.1 0.0 copy-start.9
  0.1 7.8 %first_kernel.1 = (f32[9,40,384]{2,1,0:T(8,128)S(1)}, f32[9,40,384]{2,1,0:T(8,128)S(1)}, f32[360,128]{1,0:T(8,128)S(1)}, f32[360,128]{1,0:T(8,128)S(1)}, bf16[80...) custom-call(s32[1]{0:T(128)} %bitcast.1.core, f32[9,35,384]{2,1,0:T(8,128)} %dofs.5, f32[9,9,3,384]{3,2,1,0:T(4,128)} %bitcast.6, ...), custom_call_target="tpu_custom_call" | custom-call | flops 5000000000 | bytes 1048576 | tf_op jit(solution)/shard_map/first_kernel/pallas_call | solution.py:407
  7.9 0.8 %collective-permute-start = (f32[360,128]{1,0:T(8,128)S(1)}, f32[360,128]{1,0:T(8,128)S(1)}, u32[]{:S(2)}, u32[]{:S(2)}) collective-permute-start(f32[360,128]{1,0:T(8,128)S(1)} %get-tuple-element.39), channel_id=1, source_target_pairs={{0,1},{1,0},{2,3},{3,2},{4,5},{5,4},{6,7},{7,6},{8,9},{9,8},{10,11... | collective-permute-start | bytes 552968 | tf_op jit(solution)/shard_map/ppermute | solution.py:443
  8.6 0.0 copy-done.10
  8.7 1.0 %collective-permute-done = f32[360,128]{1,0:T(8,128)S(1)} collective-permute-done((f32[360,128]{1,0:T(8,128)S(1)}, f32[360,128]{1,0:T(8,128)S(1)}, u32[]{:S(2)}, u32[]{:S(2)}) %collective-permute-start) | collective-permute-done | bytes 184352 | tf_op jit(solution)/shard_map/ppermute | solution.py:443
  9.7 6.5 %collective-permute-start.2 = (f32[360,128]{1,0:T(8,128)S(1)}, f32[360,128]{1,0:T(8,128)S(1)}, u32[]{:S(2)}, u32[]{:S(2)}) collective-permute-start(f32[360,128]{1,0:T(8,128)S(1)} %get-tuple-element.63), channel_id=1, source_target_pairs={{0,4},{1,0},{2,6},{3,2},{4,8},{5,1},{6,10},{7,3},{8,12},{9,5},{10,... | collective-permute-start | bytes 552968 | tf_op jit(solution)/shard_map/ppermute | solution.py:437
  16.2 0.9 %collective-permute-start.1 = (f32[360,128]{1,0:T(8,128)S(1)}, f32[360,128]{1,0:T(8,128)S(1)}, u32[]{:S(2)}, u32[]{:S(2)}) collective-permute-start(f32[360,128]{1,0:T(8,128)S(1)} %get-tuple-element.64), channel_id=1, source_target_pairs={{0,2},{1,0},{2,4},{3,1},{4,6},{5,3},{6,8},{7,5},{8,10},{9,7},{10,1... | collective-permute-start | bytes 552968 | tf_op jit(solution)/shard_map/ppermute | solution.py:436
  17.1 0.0 copy-done
  17.1 0.0 copy-done.1
  17.1 0.0 copy-done.2
  17.1 0.0 copy-done.3
  17.1 0.0 copy-done.4
  17.1 0.0 copy-done.5
  17.1 0.0 copy-done.6
  17.1 0.0 copy-done.7
  17.1 0.0 copy-done.8
  17.1 0.0 copy-done.9
  17.1 6.2 %second_kernel.1 = (f32[9,40,128]{2,1,0:T(8,128)S(1)}, f32[9,9,3,128]{3,2,1,0:T(4,128)S(1)}, f32[9,9,4,128]{3,2,1,0:T(4,128)S(1)}, s32[8,128]{1,0:T(8,128)S(1)},...) custom-call(s32[1]{0:T(128)} %bitcast.1.core, ...), custom_call_target="tpu_custom_call" | custom-call | flops 5000000000 | bytes 1048576 | tf_op jit(solution)/shard_map/second_kernel/pallas_call | solution.py:407
  23.4 0.0 collective-permute-done.2.b
  23.4 0.0 collective-permute-done.1.a
  23.4 0.9 %collective-permute-start.3 = (f32[360,128]{1,0:T(8,128)S(1)}, f32[360,128]{1,0:T(8,128)S(1)}, u32[]{:S(2)}, u32[]{:S(2)}) collective-permute-start(f32[360,128]{1,0:T(8,128)S(1)} %select_select_fusion.1), channel_id=1, source_target_pairs={{0,1},{1,0},{2,3},{3,2},{4,5},{5,4},{6,7},{7,6},{8,9},{9,8},{10,11... | collective-permute-start | bytes 552968 | tf_op jit(solution)/shard_map/ppermute | solution.py:443
  24.3 1.1 %collective-permute-done.3.q_in = f32[360,128]{1,0:T(8,128)S(1)} collective-permute-done((f32[360,128]{1,0:T(8,128)S(1)}, f32[360,128]{1,0:T(8,128)S(1)}, u32[]{:S(2)}, u32[]{:S(2)}) %collective-permute-start.3) | collective-permute-done | bytes 184352 | tf_op jit(solution)/shard_map/ppermute | solution.py:443
  25.4 3.4 %third_kernel.1 = (f32[9,40,128]{2,1,0:T(8,128)S(1)}, f32[9,40,128]{2,1,0:T(8,128)S(1)}, f32[360,128]{1,0:T(8,128)S(1)}, f32[360,128]{1,0:T(8,128)S(1)}) custom-call(bf16[80,256]{1,0:T(8,128)(2,1)S(1)} %get-tuple-element.38.rows, f32[360,128]{1,0:T(8,128)S(1)} %collective-permute-done.1.a, f32[360,128]{1,0:T(8,128)S(1)} %collective-permute-done.2.b, ...), custom_call_target="tpu_custom_call" | custom-call | flops 5000000000 | bytes 1048576 | tf_op jit(solution)/shard_map/third_kernel/pallas_call | solution.py:407
  28.8 0.5 collective-permute-start.4
  29.3 0.5 %spread_kernel.1 = (f32[9,40,384]{2,1,0:T(8,128)S(1)}, f32[9,40,384]{2,1,0:T(8,128)S(1)}) custom-call(f32[9,40,128]{2,1,0:T(8,128)S(1)} %get-tuple-element.49.moved_f, f32[9,40,128]{2,1,0:T(8,128)S(1)} %get-tuple-element.50.late_f, bf16[128,384]{1,0:T(8,128)(2,1)S(1)} %get-tuple-element.51.scatter, s32[1,384]{1,0:T(1,128)S(1)} %reshape.53.cluster, ...), custom_call_target="tpu_custom_call" | custom-call | flops 1000000000 | bytes 1048576 | tf_op jit(solution)/shard_map/spread_kernel/pallas_call | solution.py:407
  29.8 0.5 %collective-permute-done.4 = f32[360,128]{1,0:T(8,128)S(1)} collective-permute-done((f32[360,128]{1,0:T(8,128)S(1)}, f32[360,128]{1,0:T(8,128)S(1)}, u32[]{:S(2)}, u32[]{:S(2)}) %collective-permute-start.4) | collective-permute-done | bytes 184352 | tf_op jit(solution)/shard_map/ppermute | solution.py:443
  30.4 2.7 %collective-permute-start.6 = (f32[360,128]{1,0:T(8,128)S(1)}, f32[360,128]{1,0:T(8,128)S(1)}, u32[]{:S(2)}, u32[]{:S(2)}) collective-permute-start(f32[360,128]{1,0:T(8,128)S(1)} %get-tuple-element.61), channel_id=1, source_target_pairs={{0,4},{1,0},{2,6},{3,2},{4,8},{5,1},{6,10},{7,3},{8,12},{9,5},{10,... | collective-permute-start | bytes 552968 | tf_op jit(solution)/shard_map/ppermute | solution.py:437
  33.0 0.9 %collective-permute-start.5 = (f32[360,128]{1,0:T(8,128)S(1)}, f32[360,128]{1,0:T(8,128)S(1)}, u32[]{:S(2)}, u32[]{:S(2)}) collective-permute-start(f32[360,128]{1,0:T(8,128)S(1)} %get-tuple-element.62), channel_id=1, source_target_pairs={{0,2},{1,0},{2,4},{3,1},{4,6},{5,3},{6,8},{7,5},{8,10},{9,7},{10,1... | collective-permute-start | bytes 552968 | tf_op jit(solution)/shard_map/ppermute | solution.py:436
  33.9 6.3 %fourth_kernel.1 = (f32[9,40,384]{2,1,0:T(8,128)S(1)}, f32[360,128]{1,0:T(8,128)S(1)}) custom-call(f32[9,40,384]{2,1,0:T(8,128)S(1)} %get-tuple-element.52.start, f32[9,9,3,384]{3,2,1,0:T(4,128)S(1)} %bitcast.8, f32[9,9,4,384]{3,2,1,0:T(4,128)S(1)} %bitcast.10, f32[9,9,4,384]{3,2,1,0:T(4,128)S(1)} %bitcast.12, s32[1,384]{1,0:T(1,128)S(1)} %reshape.53.cluster, ...), custom_call_target="tpu_custom_call" | custom-call | flops 5000000000 | bytes 1048576 | tf_op jit(solution)/shard_map/fourth_kernel/pallas_call | solution.py:407
  40.3 0.0 collective-permute-done.6.b
  40.3 0.0 collective-permute-done.5.a
  40.3 0.1 select_select_fusion
  40.4 2.8 %collective-permute-start.7 = (f32[360,128]{1,0:T(8,128)S(1)}, f32[360,128]{1,0:T(8,128)S(1)}, u32[]{:S(2)}, u32[]{:S(2)}) collective-permute-start(f32[360,128]{1,0:T(8,128)S(1)} %select_select_fusion), channel_id=1, source_target_pairs={{0,1},{1,0},{2,3},{3,2},{4,5},{5,4},{6,7},{7,6},{8,9},{9,8},{10,11... | collective-permute-start | bytes 552968 | tf_op jit(solution)/shard_map/ppermute | solution.py:443
  43.2 1.1 %collective-permute-done.7.q_in = f32[360,128]{1,0:T(8,128)S(1)} collective-permute-done((f32[360,128]{1,0:T(8,128)S(1)}, f32[360,128]{1,0:T(8,128)S(1)}, u32[]{:S(2)}, u32[]{:S(2)}) %collective-permute-start.7) | collective-permute-done | bytes 184352 | tf_op jit(solution)/shard_map/ppermute | solution.py:443
  44.2 3.9 %fifth_kernel.1 = f32[9,35,384]{2,1,0:T(8,128)} custom-call(f32[9,35,384]{2,1,0:T(8,128)S(1)} %copy-done, f32[9,9,4,384]{3,2,1,0:T(4,128)S(1)} %bitcast.13, s32[1,384]{1,0:T(1,128)S(1)} %reshape.53.cluster, s32[4,384]{1,0:T(4,128)S(1)} %get-tuple-element.37.nb_all, s32[4,384]{1,0:T(4,128)S(1)} %copy-done.9, f32[9,40,384]{2,1,0:T(8,128)S(1)} %get-tuple-element.58.partial, ...), custom_call_target="tpu_custom_call" | custom-call | flops 5000000000 | bytes 1048576 | tf_op jit(solution)/shard_map/fifth_kernel/pallas_call | solution.py:407
  (6 shorter events, 0.1 us)
Async XLA Ops:
  0.0 8.7 %copy-start.10 = (s32[384]{0:T(512)S(1)}, s32[384]{0:T(512)}, u32[]{:S(2)}) copy-start(s32[384]{0:T(512)} %param.16) | copy-start | bytes 4612
  0.0 17.1 %copy-start = (f32[9,35,384]{2,1,0:T(8,128)S(1)}, f32[9,35,384]{2,1,0:T(8,128)}, u32[]{:S(2)}) copy-start(f32[9,35,384]{2,1,0:T(8,128)} %dofs.5) | copy-start | bytes 1451524
  0.0 17.1 %copy-start.1 = (f32[3,9,9,384]{3,0,2,1:T(4,128)S(1)}, f32[3,9,9,384]{3,0,2,1:T(4,128)}, u32[]{:S(2)}) copy-start(f32[3,9,9,384]{3,0,2,1:T(4,128)} %param.13) | copy-start | bytes 1119748
  0.0 17.1 %copy-start.2 = (f32[4,9,9,384]{3,0,2,1:T(4,128)S(1)}, f32[4,9,9,384]{3,0,2,1:T(4,128)}, u32[]{:S(2)}) copy-start(f32[4,9,9,384]{3,0,2,1:T(4,128)} %param.14) | copy-start | bytes 1492996
  0.0 17.1 %copy-start.3 = (f32[4,9,9,384]{3,0,2,1:T(4,128)S(1)}, f32[4,9,9,384]{3,0,2,1:T(4,128)}, u32[]{:S(2)}) copy-start(f32[4,9,9,384]{3,0,2,1:T(4,128)} %param.15) | copy-start | bytes 1492996
  0.0 17.1 %copy-start.4 = (f32[3,35,35]{2,1,0:T(8,128)S(1)}, f32[3,35,35]{2,1,0:T(8,128)}, u32[]{:S(2)}) copy-start(f32[3,35,35]{2,1,0:T(8,128)} %stiffness.1) | copy-start | bytes 44104
  0.0 17.1 %copy-start.5 = (f32[4,15,35]{2,0,1:T(4,128)S(1)}, f32[4,15,35]{2,0,1:T(4,128)}, u32[]{:S(2)}) copy-start(f32[4,15,35]{2,0,1:T(4,128)} %param.21) | copy-start | bytes 25204
  0.0 17.1 %copy-start.6 = (f32[4,35,15]{1,0,2:T(4,128)S(1)}, f32[4,35,15]{1,0,2:T(4,128)}, u32[]{:S(2)}) copy-start(f32[4,35,15]{1,0,2:T(4,128)} %param.22) | copy-start | bytes 25204
  0.1 17.1 %copy-start.7 = (f32[3,15,15]{2,1,0:T(8,128)S(1)}, f32[3,15,15]{2,1,0:T(8,128)}, u32[]{:S(2)}) copy-start(f32[3,15,15]{2,1,0:T(8,128)} %turn.1) | copy-start | bytes 8104
  0.1 17.1 %copy-start.8 = (s32[4,384]{1,0:T(4,128)S(1)}, s32[4,384]{1,0:T(4,128)}, u32[]{:S(2)}) copy-start(s32[4,384]{1,0:T(4,128)} %neighbour.1) | copy-start | bytes 18436
  0.1 17.1 %copy-start.9 = (s32[4,384]{1,0:T(4,128)S(1)}, s32[4,384]{1,0:T(4,128)}, u32[]{:S(2)}) copy-start(s32[4,384]{1,0:T(4,128)} %codes.5) | copy-start | bytes 18436
  7.9 1.8 %collective-permute-start = (f32[360,128]{1,0:T(8,128)S(1)}, f32[360,128]{1,0:T(8,128)S(1)}, u32[]{:S(2)}, u32[]{:S(2)}) collective-permute-start(f32[360,128]{1,0:T(8,128)S(1)} %get-tuple-element.39), channel_id=1, source_target_pairs={{0,1},{1,0},{2,3},{3,2},{4,5},{5,4},{6,7},{7,6},{8,9},{9,8},{10,11... | collective-permute-start | bytes 552968 | tf_op jit(solution)/shard_map/ppermute | solution.py:443
  9.7 13.6 %collective-permute-start.2 = (f32[360,128]{1,0:T(8,128)S(1)}, f32[360,128]{1,0:T(8,128)S(1)}, u32[]{:S(2)}, u32[]{:S(2)}) collective-permute-start(f32[360,128]{1,0:T(8,128)S(1)} %get-tuple-element.63), channel_id=1, source_target_pairs={{0,4},{1,0},{2,6},{3,2},{4,8},{5,1},{6,10},{7,3},{8,12},{9,5},{10,... | collective-permute-start | bytes 552968 | tf_op jit(solution)/shard_map/ppermute | solution.py:437
  16.2 7.2 %collective-permute-start.1 = (f32[360,128]{1,0:T(8,128)S(1)}, f32[360,128]{1,0:T(8,128)S(1)}, u32[]{:S(2)}, u32[]{:S(2)}) collective-permute-start(f32[360,128]{1,0:T(8,128)S(1)} %get-tuple-element.64), channel_id=1, source_target_pairs={{0,2},{1,0},{2,4},{3,1},{4,6},{5,3},{6,8},{7,5},{8,10},{9,7},{10,1... | collective-permute-start | bytes 552968 | tf_op jit(solution)/shard_map/ppermute | solution.py:436
  23.4 1.9 %collective-permute-start.3 = (f32[360,128]{1,0:T(8,128)S(1)}, f32[360,128]{1,0:T(8,128)S(1)}, u32[]{:S(2)}, u32[]{:S(2)}) collective-permute-start(f32[360,128]{1,0:T(8,128)S(1)} %select_select_fusion.1), channel_id=1, source_target_pairs={{0,1},{1,0},{2,3},{3,2},{4,5},{5,4},{6,7},{7,6},{8,9},{9,8},{10,11... | collective-permute-start | bytes 552968 | tf_op jit(solution)/shard_map/ppermute | solution.py:443
  28.8 1.5 %collective-permute-start.4 = (f32[360,128]{1,0:T(8,128)S(1)}, f32[360,128]{1,0:T(8,128)S(1)}, u32[]{:S(2)}, u32[]{:S(2)}) collective-permute-start(f32[360,128]{1,0:T(8,128)S(1)} %get-tuple-element.59), channel_id=1, source_target_pairs={{0,1},{1,0},{2,3},{3,2},{4,5},{5,4},{6,7},{7,6},{8,9},{9,8},{10,11... | collective-permute-start | bytes 552968 | tf_op jit(solution)/shard_map/ppermute | solution.py:443
  30.4 9.9 %collective-permute-start.6 = (f32[360,128]{1,0:T(8,128)S(1)}, f32[360,128]{1,0:T(8,128)S(1)}, u32[]{:S(2)}, u32[]{:S(2)}) collective-permute-start(f32[360,128]{1,0:T(8,128)S(1)} %get-tuple-element.61), channel_id=1, source_target_pairs={{0,4},{1,0},{2,6},{3,2},{4,8},{5,1},{6,10},{7,3},{8,12},{9,5},{10,... | collective-permute-start | bytes 552968 | tf_op jit(solution)/shard_map/ppermute | solution.py:437
  33.0 7.2 %collective-permute-start.5 = (f32[360,128]{1,0:T(8,128)S(1)}, f32[360,128]{1,0:T(8,128)S(1)}, u32[]{:S(2)}, u32[]{:S(2)}) collective-permute-start(f32[360,128]{1,0:T(8,128)S(1)} %get-tuple-element.62), channel_id=1, source_target_pairs={{0,2},{1,0},{2,4},{3,1},{4,6},{5,3},{6,8},{7,5},{8,10},{9,7},{10,1... | collective-permute-start | bytes 552968 | tf_op jit(solution)/shard_map/ppermute | solution.py:436
  40.4 3.9 %collective-permute-start.7 = (f32[360,128]{1,0:T(8,128)S(1)}, f32[360,128]{1,0:T(8,128)S(1)}, u32[]{:S(2)}, u32[]{:S(2)}) collective-permute-start(f32[360,128]{1,0:T(8,128)S(1)} %select_select_fusion), channel_id=1, source_target_pairs={{0,1},{1,0},{2,3},{3,2},{4,5},{5,4},{6,7},{7,6},{8,9},{9,8},{10,11... | collective-permute-start | bytes 552968 | tf_op jit(solution)/shard_map/ppermute | solution.py:443

commit v4 on v3

--- a/solution.py
+++ b/solution.py
@@ -1,3 +1,4 @@
+import functools
 import math
 
 import jax
@@ -88,7 +89,7 @@
     return jnp.concatenate([x, jnp.zeros((8, x.shape[1]), F32)], axis=0)
 
 
-def star_times(star_ref, source, p, width):
+def star_times(star_ref, source, width, p):
     columns = []
     for at in lanes_of(width):
         values = [source[q, :, at] for q in range(Q)]
@@ -108,11 +109,23 @@
     return out[:C] + out[C:]
 
 
+PAIRS = ((0, 1), (2, 3), (4, 5), (6, 7), (8,))
+
+
+def in_pairs(left, right_of, width):
+    for group in PAIRS:
+        right = [right_of(p) for p in group]
+        out = mxu(left, jnp.concatenate(right, axis=1) if len(right) > 1 else right[0])
+        for at, p in enumerate(group):
+            yield p, out[:, at * width : (at + 1) * width]
+
+
 def taylor(star_ref, rows, cur_ref, width, add):
     for level in range(ORDER - 1):
         source, target = cur_ref.at[level % 2], cur_ref.at[(level + 1) % 2]
-        for p in range(Q):
-            value = halves(mxu(rows, star_times(star_ref, source, p, width)))
+        right_of = functools.partial(star_times, star_ref, source, width)
+        for p, out in in_pairs(rows, right_of, width):
+            value = halves(out)
             target[p] = value
             add(level, p, value)
 
@@ -131,9 +144,20 @@
                 target[p, rows, at] = total
 
 
+def lifted(lift_rows, flow, width):
+    return in_pairs(lift_rows, lambda p: three_parts(flow[p]), width)
+
+
+def advance(out_ref, start, star_ref, own, flow, volume_rows, lift_rows, width):
+    right_of = functools.partial(star_times, star_ref, own, width)
+    volume = in_pairs(volume_rows, right_of, width)
+    for (p, inside), (_, faces) in zip(volume, lifted(lift_rows, flow, width)):
+        out_ref[p] = start[p] + halves(inside) + faces
+
+
 def own_faces(own, proj_rows, face_ref, width):
-    for q in range(Q):
-        face_ref[q] = mxu(proj_rows, three_parts(padded48(own[q])))
+    for q, out in in_pairs(proj_rows, lambda q: three_parts(padded48(own[q])), width):
+        face_ref[q] = out
 
 
 def beside(rows):
@@ -154,10 +178,23 @@
     return total
 
 
-def near_faces(near_ref, codes, turn_rows, face_ref, width):
+def ghost_pick(neighbour, width):
+    hit = iota((GHOST, 4 * width), 0) + E == beside(neighbour)
+    return jnp.where(hit, 1.0, 0.0).astype(BF16)
+
+
+def near_parts(near_refs, q):
+    values = [padded48(ref[q * C : (q + 1) * C, :]) for ref in near_refs]
+    if len(values) == 1:
+        return three_parts(values[0])
+    high, low = [value.astype(BF16) for value in values]
+    return jnp.concatenate([high, low, high], axis=0)
+
+
+def near_faces(near_refs, codes, turn_rows, face_ref, width):
     code = beside(codes)
     for q in range(Q):
-        every = mxu(turn_rows, three_parts(padded48(near_ref[q * C : (q + 1) * C, :])))
+        every = mxu(turn_rows, near_parts(near_refs, q))
         chosen = every[0:G]
         for k in range(1, 12):
             chosen = jnp.where(code == k, every[k * G : (k + 1) * G], chosen)
@@ -300,18 +337,13 @@
     flux(minus_f, face, flow, F, False)
     parts = split(flat(early[...]))
     near[...] = gathered([(parts, 0, None)], nb, F)
-    near_faces(near, code, turn_rows[...], face, F)
+    near_faces([near], code, turn_rows[...], face, F)
     flux(plus_f, face, flow, F, True)
     near_medium[...] = gathered([(parts, 0, kinds == 1)], table, E)
     steady[...] = both(jnp.where(kinds == 0, 0.0, flat(later[...])), pick[...])
     route[...] = mxu(picks, pick[...]).astype(BF16)
 
-    for p in range(Q):
-        field[p] = (
-            field[p]
-            + halves(mxu(volume_rows[...], star_times(star_f, early_f, p, F)))
-            + mxu(lift_rows[...], three_parts(flow[p]))
-        )
+    advance(field, field, star_f, early_f, flow, volume_rows[...], lift_rows[...], F)
 
 
 def third_kernel(
@@ -319,12 +351,13 @@
     moved_f, late_f, inner, outer,
     cur, face, flow, near,
 ):
-    ghosts = split(ghost_array(a, b, q_in))
-    near[...] = gathered([(ghosts, E, None)], lines_f[0:4, :], F)
-    near_faces(near, lines_f[4:8, :], turn_rows[...], face, F)
+    columns = ghost_pick(lines_f[0:4, :], F)
+    for at, part in enumerate(split(ghost_array(a, b, q_in))):
+        near[at] = mxu(part, columns)
+    near_faces([near.at[0], near.at[1]], lines_f[4:8, :], turn_rows[...], face, F)
     flux(plus_f, face, flow, F, False)
-    for p in range(Q):
-        value = field[p] + mxu(lift_rows[...], three_parts(flow[p]))
+    for p, faces in lifted(lift_rows[...], flow, F):
+        value = field[p] + faces
         cur[0, p] = value
         moved_f[p] = value
         late_f[p] = value
@@ -338,7 +371,8 @@
     outer[...] = sent[:, LANES:]
 
 
-def spread_kernel(moved_f, late_f, scatter, cluster, later, dofs, start, late):
+def spread_kernel(moved_f, late_f, scatter, cluster, later, dofs, nb_all, start, late, columns):
+    columns[...] = ghost_pick(nb_all[...], E)
     fast = cluster[...] == 0
     moved = both(flat(moved_f[...]), scatter[...])
     fresh = both(flat(late_f[...]), scatter[...])
@@ -372,27 +406,22 @@
         (split(ghost_array(a, b, q_in)), E, kinds == 1),
     ]
     near[...] = gathered(parts, nb_all[...], E, near_medium[...])
-    near_faces(near, codes[...], turn_rows[...], face, E)
+    near_faces([near], codes[...], turn_rows[...], face, E)
     flux(plus, face, flow, E, True)
-    for p in range(Q):
-        out[p] = (
-            start[p]
-            + halves(mxu(volume_rows[...], star_times(star, own, p, E)))
-            + mxu(lift_rows[...], three_parts(flow[p]))
-        )
+    advance(out, start, star, own, flow, volume_rows[...], lift_rows[...], E)
 
 
 def fifth_kernel(
-    dofs, plus, cluster, nb_all, codes, partial, a, b, q_in, lift_rows, turn_rows,
+    dofs, plus, cluster, columns, codes, partial, a, b, q_in, lift_rows, turn_rows,
     out, face, flow, near,
 ):
-    ghosts = split(ghost_array(a, b, q_in))
-    near[...] = gathered([(ghosts, E, None)], nb_all[...], E)
-    near_faces(near, codes[...], turn_rows[...], face, E)
+    for at, part in enumerate(split(ghost_array(a, b, q_in))):
+        near[at] = mxu(part, columns[...])
+    near_faces([near.at[0], near.at[1]], codes[...], turn_rows[...], face, E)
     flux(plus, face, flow, E, False)
     active = cluster[...] < 2
-    for p in range(Q):
-        value = partial[p] + mxu(lift_rows[...], three_parts(flow[p]))
+    for p, faces in lifted(lift_rows[...], flow, E):
+        value = partial[p] + faces
         out[p] = jnp.where(active, value[0:35], dofs[p])
 
 
@@ -513,14 +542,14 @@
             rows, a, b, q_in, field, star_f, plus_f, lines_f, steady, route, lift_rows, turn_rows
         ],
         [
-            ((2,) + compact, F32), ((Q, 64, F), F32), ((Q, 64, F), F32), ((Q * C, 4 * F), F32),
+            ((2,) + compact, F32), ((Q, 64, F), F32), ((Q, 64, F), F32), ((2, Q * C, 4 * F), F32),
         ],
     )
     a2, b2 = to_chips(inner, outer)
-    start, late = call(
+    start, late, columns = call(
         spread_kernel,
-        [(whole, F32), (whole, F32)],
-        [moved_f, late_f, scatter, cluster, later, dofs],
+        [(whole, F32), (whole, F32), ((GHOST, 4 * E), BF16)],
+        [moved_f, late_f, scatter, cluster, later, dofs, nb_all],
         [],
         micros=1,
     )
@@ -537,8 +566,8 @@
     (out,) = call(
         fifth_kernel,
         [((Q, 35, E), F32)],
-        [dofs, flux_plus, cluster, nb_all, face_code, partial, a2, b2, q2, lift_rows, turn_rows],
-        [((Q, 64, E), F32), ((Q, 64, E), F32), ((Q * C, 4 * E), F32)],
+        [dofs, flux_plus, cluster, columns, face_code, partial, a2, b2, q2, lift_rows, turn_rows],
+        [((Q, 64, E), F32), ((Q, 64, E), F32), ((2, Q * C, 4 * E), F32)],
     )
     return out
 

time: 48.3 us -> 50 us (1.035)
  starting transfers between devices: 15.8 us -> 17.8 us
    ppermute x2, starting transfers between devices: 9.16 us -> 0.52 us  [to_chips(): b = lax.ppermute(jnp.where(first, outer, beside), 'dom', along(2))]
    ppermute x2, starting transfers between devices: 1.76 us -> 8.92 us  [to_chips(): a = lax.ppermute(jnp.where(first, beside, outer), 'dom', along(1))]
    ppermute x4, starting transfers between devices: 4.91 us -> 8.37 us  [to_pair(): lax.ppermute(value, 'dom', [(device, device ^ 1) for device in range(coun...]
  transfers between devices with their start and end apart: 8 -> 8, of which waited for: 4 -> 4; matrix products, arithmetic and copies ran while one was open for 0% -> 0% of each run, Pallas kernels for 27% -> 26%
where the time goes in v4:
time: 50 us; the launch traced here: 49.9 us
  Pallas kernels  28.2 us (56%)
  starting transfers between devices  17.8 us (36%)
  waiting for transfers between devices  3.5 us (7%)
    pallas_call x6, Pallas kernels, call(): pl.pallas_call(kernel, out_shape=[jax.ShapeDtypeStruct(*o) for o in outs]...  28.2 us
    ppermute x2, starting transfers between devices, to_chips(): a = lax.ppermute(jnp.where(first, beside, outer), 'dom', along(1))  8.92 us
    ppermute x4, starting transfers between devices, to_pair(): lax.ppermute(value, 'dom', [(device, device ^ 1) for device in range(coun...  8.37 us
    ppermute x4, waiting for transfers between devices, to_pair(): lax.ppermute(value, 'dom', [(device, device ^ 1) for device in range(coun...  3.49 us
  transfers between devices with their start and end apart: 8, of which 4 were waited for; matrix products, arithmetic and copies ran while one was open for 0% of the time, Pallas kernels for 26%

profile of v4, /device:TPU:25, one launch (start us, length us, event | category | flops | bytes accessed | tf_op | source)
XLA Modules:
  0.0 49.9 jit_solution(3249477382029825850)
XLA Ops:
  0.0 0.0 copy-start.10
  0.0 0.0 copy-start
  0.0 0.0 copy-start.1
  0.0 0.0 copy-start.2
  0.0 0.0 copy-start.3
  0.0 0.0 copy-start.4
  0.0 0.0 copy-start.5
  0.0 0.0 copy-start.6
  0.1 0.0 copy-start.7
  0.1 0.0 copy-start.8
  0.1 0.0 copy-start.9
  0.1 7.9 %first_kernel.1 = (f32[9,40,384]{2,1,0:T(8,128)S(1)}, f32[9,40,384]{2,1,0:T(8,128)S(1)}, f32[360,128]{1,0:T(8,128)S(1)}, f32[360,128]{1,0:T(8,128)S(1)}, bf16[80...) custom-call(s32[1]{0:T(128)} %bitcast.1.core, f32[9,35,384]{2,1,0:T(8,128)} %dofs.5, f32[9,9,3,384]{3,2,1,0:T(4,128)} %bitcast.6, ...), custom_call_target="tpu_custom_call" | custom-call | flops 5000000000 | bytes 1048576 | tf_op jit(solution)/shard_map/first_kernel/pallas_call | solution.py:436
  8.0 0.8 %collective-permute-start = (f32[360,128]{1,0:T(8,128)S(1)}, f32[360,128]{1,0:T(8,128)S(1)}, u32[]{:S(2)}, u32[]{:S(2)}) collective-permute-start(f32[360,128]{1,0:T(8,128)S(1)} %get-tuple-element.35), channel_id=1, source_target_pairs={{0,1},{1,0},{2,3},{3,2},{4,5},{5,4},{6,7},{7,6},{8,9},{9,8},{10,11... | collective-permute-start | bytes 552968 | tf_op jit(solution)/shard_map/ppermute | solution.py:472
  8.8 0.0 copy-done.10
  8.8 1.0 %collective-permute-done = f32[360,128]{1,0:T(8,128)S(1)} collective-permute-done((f32[360,128]{1,0:T(8,128)S(1)}, f32[360,128]{1,0:T(8,128)S(1)}, u32[]{:S(2)}, u32[]{:S(2)}) %collective-permute-start) | collective-permute-done | bytes 184352 | tf_op jit(solution)/shard_map/ppermute | solution.py:472
  9.9 6.2 %collective-permute-start.1 = (f32[360,128]{1,0:T(8,128)S(1)}, f32[360,128]{1,0:T(8,128)S(1)}, u32[]{:S(2)}, u32[]{:S(2)}) collective-permute-start(f32[360,128]{1,0:T(8,128)S(1)} %get-tuple-element.66), channel_id=1, source_target_pairs={{0,2},{1,0},{2,4},{3,1},{4,6},{5,3},{6,8},{7,5},{8,10},{9,7},{10,1... | collective-permute-start | bytes 552968 | tf_op jit(solution)/shard_map/ppermute | solution.py:465
  16.1 0.5 %collective-permute-start.2 = (f32[360,128]{1,0:T(8,128)S(1)}, f32[360,128]{1,0:T(8,128)S(1)}, u32[]{:S(2)}, u32[]{:S(2)}) collective-permute-start(f32[360,128]{1,0:T(8,128)S(1)} %get-tuple-element.65), channel_id=1, source_target_pairs={{0,4},{1,0},{2,6},{3,2},{4,8},{5,1},{6,10},{7,3},{8,12},{9,5},{10,... | collective-permute-start | bytes 552968 | tf_op jit(solution)/shard_map/ppermute | solution.py:466
  16.6 0.0 copy-done
  16.6 0.0 copy-done.1
  16.6 0.0 copy-done.2
  16.6 0.0 copy-done.3
  16.6 0.0 copy-done.4
  16.6 0.0 copy-done.5
  16.6 0.0 copy-done.6
  16.6 0.0 copy-done.7
  16.6 0.0 copy-done.8
  16.7 0.0 copy-done.9
  16.7 6.1 %second_kernel.1 = (f32[9,40,128]{2,1,0:T(8,128)S(1)}, f32[9,9,3,128]{3,2,1,0:T(4,128)S(1)}, f32[9,9,4,128]{3,2,1,0:T(4,128)S(1)}, s32[8,128]{1,0:T(8,128)S(1)},...) custom-call(s32[1]{0:T(128)} %bitcast.1.core, ...), custom_call_target="tpu_custom_call" | custom-call | flops 5000000000 | bytes 1048576 | tf_op jit(solution)/shard_map/second_kernel/pallas_call | solution.py:436
  22.8 0.0 collective-permute-done.1.a
  22.8 0.0 collective-permute-done.2.b
  22.8 3.1 %collective-permute-start.3 = (f32[360,128]{1,0:T(8,128)S(1)}, f32[360,128]{1,0:T(8,128)S(1)}, u32[]{:S(2)}, u32[]{:S(2)}) collective-permute-start(f32[360,128]{1,0:T(8,128)S(1)} %select_select_fusion.1), channel_id=1, source_target_pairs={{0,1},{1,0},{2,3},{3,2},{4,5},{5,4},{6,7},{7,6},{8,9},{9,8},{10,11... | collective-permute-start | bytes 552968 | tf_op jit(solution)/shard_map/ppermute | solution.py:472
  25.9 1.1 %collective-permute-done.3.q_in = f32[360,128]{1,0:T(8,128)S(1)} collective-permute-done((f32[360,128]{1,0:T(8,128)S(1)}, f32[360,128]{1,0:T(8,128)S(1)}, u32[]{:S(2)}, u32[]{:S(2)}) %collective-permute-start.3) | collective-permute-done | bytes 184352 | tf_op jit(solution)/shard_map/ppermute | solution.py:472
  27.0 3.4 %third_kernel.1 = (f32[9,40,128]{2,1,0:T(8,128)S(1)}, f32[9,40,128]{2,1,0:T(8,128)S(1)}, f32[360,128]{1,0:T(8,128)S(1)}, f32[360,128]{1,0:T(8,128)S(1)}) custom-call(bf16[80,256]{1,0:T(8,128)(2,1)S(1)} %get-tuple-element.34.rows, f32[360,128]{1,0:T(8,128)S(1)} %collective-permute-done.1.a, f32[360,128]{1,0:T(8,128)S(1)} %collective-permute-done.2.b, ...), custom_call_target="tpu_custom_call" | custom-call | flops 5000000000 | bytes 1048576 | tf_op jit(solution)/shard_map/third_kernel/pallas_call | solution.py:436
  30.4 0.4 collective-permute-start.4
  30.8 0.7 %spread_kernel.1 = (f32[9,40,384]{2,1,0:T(8,128)S(1)}, f32[9,40,384]{2,1,0:T(8,128)S(1)}, bf16[256,1536]{1,0:T(8,128)(2,1)S(1)}) custom-call(f32[9,40,128]{2,1,0:T(8,128)S(1)} %get-tuple-element.49.moved_f, f32[9,40,128]{2,1,0:T(8,128)S(1)} %get-tuple-element.50.late_f, bf16[128,384]{1,0:T(8,128)(2,1)S(1)} %get-tuple-element.51.scatter, ...), custom_call_target="tpu_custom_call" | custom-call | flops 1000000000 | bytes 1048576 | tf_op jit(solution)/shard_map/spread_kernel/pallas_call | solution.py:436
  31.5 0.3 collective-permute-done.4
  31.9 2.7 %collective-permute-start.5 = (f32[360,128]{1,0:T(8,128)S(1)}, f32[360,128]{1,0:T(8,128)S(1)}, u32[]{:S(2)}, u32[]{:S(2)}) collective-permute-start(f32[360,128]{1,0:T(8,128)S(1)} %get-tuple-element.64), channel_id=1, source_target_pairs={{0,2},{1,0},{2,4},{3,1},{4,6},{5,3},{6,8},{7,5},{8,10},{9,7},{10,1... | collective-permute-start | bytes 552968 | tf_op jit(solution)/shard_map/ppermute | solution.py:465
  34.6 0.0 collective-permute-start.6
  34.6 6.2 %fourth_kernel.1 = (f32[9,40,384]{2,1,0:T(8,128)S(1)}, f32[360,128]{1,0:T(8,128)S(1)}) custom-call(f32[9,40,384]{2,1,0:T(8,128)S(1)} %get-tuple-element.54.start, f32[9,9,3,384]{3,2,1,0:T(4,128)S(1)} %bitcast.8, f32[9,9,4,384]{3,2,1,0:T(4,128)S(1)} %bitcast.10, f32[9,9,4,384]{3,2,1,0:T(4,128)S(1)} %bitcast.12, s32[1,384]{1,0:T(1,128)S(1)} %reshape.53.cluster, ...), custom_call_target="tpu_custom_call" | custom-call | flops 5000000000 | bytes 1048576 | tf_op jit(solution)/shard_map/fourth_kernel/pallas_call | solution.py:436
  40.9 0.0 collective-permute-done.5.a
  40.9 0.0 collective-permute-done.6.b
  40.9 4.1 %collective-permute-start.7 = (f32[360,128]{1,0:T(8,128)S(1)}, f32[360,128]{1,0:T(8,128)S(1)}, u32[]{:S(2)}, u32[]{:S(2)}) collective-permute-start(f32[360,128]{1,0:T(8,128)S(1)} %select_select_fusion), channel_id=1, source_target_pairs={{0,1},{1,0},{2,3},{3,2},{4,5},{5,4},{6,7},{7,6},{8,9},{9,8},{10,11... | collective-permute-start | bytes 552968 | tf_op jit(solution)/shard_map/ppermute | solution.py:472
  45.0 1.1 %collective-permute-done.7.q_in = f32[360,128]{1,0:T(8,128)S(1)} collective-permute-done((f32[360,128]{1,0:T(8,128)S(1)}, f32[360,128]{1,0:T(8,128)S(1)}, u32[]{:S(2)}, u32[]{:S(2)}) %collective-permute-start.7) | collective-permute-done | bytes 184352 | tf_op jit(solution)/shard_map/ppermute | solution.py:472
  46.0 3.8 %fifth_kernel.1 = f32[9,35,384]{2,1,0:T(8,128)} custom-call(f32[9,35,384]{2,1,0:T(8,128)S(1)} %copy-done, f32[9,9,4,384]{3,2,1,0:T(4,128)S(1)} %bitcast.13, s32[1,384]{1,0:T(1,128)S(1)} %reshape.53.cluster, bf16[256,1536]{1,0:T(8,128)(2,1)S(1)} %get-tuple-element.53.columns, s32[4,384]{1,0:T(4,128)S(1)} %copy-done.9, ...), custom_call_target="tpu_custom_call" | custom-call | flops 5000000000 | bytes 1048576 | tf_op jit(solution)/shard_map/fifth_kernel/pallas_call | solution.py:436
  (7 shorter events, 0.1 us)
Async XLA Ops:
  0.0 8.8 %copy-start.10 = (s32[384]{0:T(512)S(1)}, s32[384]{0:T(512)}, u32[]{:S(2)}) copy-start(s32[384]{0:T(512)} %param.16) | copy-start | bytes 4612
  0.0 16.6 %copy-start = (f32[9,35,384]{2,1,0:T(8,128)S(1)}, f32[9,35,384]{2,1,0:T(8,128)}, u32[]{:S(2)}) copy-start(f32[9,35,384]{2,1,0:T(8,128)} %dofs.5) | copy-start | bytes 1451524
  0.0 16.6 %copy-start.1 = (f32[3,9,9,384]{3,0,2,1:T(4,128)S(1)}, f32[3,9,9,384]{3,0,2,1:T(4,128)}, u32[]{:S(2)}) copy-start(f32[3,9,9,384]{3,0,2,1:T(4,128)} %param.13) | copy-start | bytes 1119748
  0.0 16.6 %copy-start.2 = (f32[4,9,9,384]{3,0,2,1:T(4,128)S(1)}, f32[4,9,9,384]{3,0,2,1:T(4,128)}, u32[]{:S(2)}) copy-start(f32[4,9,9,384]{3,0,2,1:T(4,128)} %param.14) | copy-start | bytes 1492996
  0.0 16.6 %copy-start.3 = (f32[4,9,9,384]{3,0,2,1:T(4,128)S(1)}, f32[4,9,9,384]{3,0,2,1:T(4,128)}, u32[]{:S(2)}) copy-start(f32[4,9,9,384]{3,0,2,1:T(4,128)} %param.15) | copy-start | bytes 1492996
  0.0 16.6 %copy-start.4 = (f32[3,35,35]{2,1,0:T(8,128)S(1)}, f32[3,35,35]{2,1,0:T(8,128)}, u32[]{:S(2)}) copy-start(f32[3,35,35]{2,1,0:T(8,128)} %stiffness.1) | copy-start | bytes 44104
  0.0 16.6 %copy-start.5 = (f32[4,15,35]{2,0,1:T(4,128)S(1)}, f32[4,15,35]{2,0,1:T(4,128)}, u32[]{:S(2)}) copy-start(f32[4,15,35]{2,0,1:T(4,128)} %param.21) | copy-start | bytes 25204
  0.0 16.6 %copy-start.6 = (f32[4,35,15]{1,0,2:T(4,128)S(1)}, f32[4,35,15]{1,0,2:T(4,128)}, u32[]{:S(2)}) copy-start(f32[4,35,15]{1,0,2:T(4,128)} %param.22) | copy-start | bytes 25204
  0.1 16.6 %copy-start.7 = (f32[3,15,15]{2,1,0:T(8,128)S(1)}, f32[3,15,15]{2,1,0:T(8,128)}, u32[]{:S(2)}) copy-start(f32[3,15,15]{2,1,0:T(8,128)} %turn.1) | copy-start | bytes 8104
  0.1 16.6 %copy-start.8 = (s32[4,384]{1,0:T(4,128)S(1)}, s32[4,384]{1,0:T(4,128)}, u32[]{:S(2)}) copy-start(s32[4,384]{1,0:T(4,128)} %neighbour.1) | copy-start | bytes 18436
  0.1 16.6 %copy-start.9 = (s32[4,384]{1,0:T(4,128)S(1)}, s32[4,384]{1,0:T(4,128)}, u32[]{:S(2)}) copy-start(s32[4,384]{1,0:T(4,128)} %codes.5) | copy-start | bytes 18436
  8.0 1.8 %collective-permute-start = (f32[360,128]{1,0:T(8,128)S(1)}, f32[360,128]{1,0:T(8,128)S(1)}, u32[]{:S(2)}, u32[]{:S(2)}) collective-permute-start(f32[360,128]{1,0:T(8,128)S(1)} %get-tuple-element.35), channel_id=1, source_target_pairs={{0,1},{1,0},{2,3},{3,2},{4,5},{5,4},{6,7},{7,6},{8,9},{9,8},{10,11... | collective-permute-start | bytes 552968 | tf_op jit(solution)/shard_map/ppermute | solution.py:472
  9.9 12.9 %collective-permute-start.1 = (f32[360,128]{1,0:T(8,128)S(1)}, f32[360,128]{1,0:T(8,128)S(1)}, u32[]{:S(2)}, u32[]{:S(2)}) collective-permute-start(f32[360,128]{1,0:T(8,128)S(1)} %get-tuple-element.66), channel_id=1, source_target_pairs={{0,2},{1,0},{2,4},{3,1},{4,6},{5,3},{6,8},{7,5},{8,10},{9,7},{10,1... | collective-permute-start | bytes 552968 | tf_op jit(solution)/shard_map/ppermute | solution.py:465
  16.1 6.7 %collective-permute-start.2 = (f32[360,128]{1,0:T(8,128)S(1)}, f32[360,128]{1,0:T(8,128)S(1)}, u32[]{:S(2)}, u32[]{:S(2)}) collective-permute-start(f32[360,128]{1,0:T(8,128)S(1)} %get-tuple-element.65), channel_id=1, source_target_pairs={{0,4},{1,0},{2,6},{3,2},{4,8},{5,1},{6,10},{7,3},{8,12},{9,5},{10,... | collective-permute-start | bytes 552968 | tf_op jit(solution)/shard_map/ppermute | solution.py:466
  22.8 4.2 %collective-permute-start.3 = (f32[360,128]{1,0:T(8,128)S(1)}, f32[360,128]{1,0:T(8,128)S(1)}, u32[]{:S(2)}, u32[]{:S(2)}) collective-permute-start(f32[360,128]{1,0:T(8,128)S(1)} %select_select_fusion.1), channel_id=1, source_target_pairs={{0,1},{1,0},{2,3},{3,2},{4,5},{5,4},{6,7},{7,6},{8,9},{9,8},{10,11... | collective-permute-start | bytes 552968 | tf_op jit(solution)/shard_map/ppermute | solution.py:472
  30.4 1.5 %collective-permute-start.4 = (f32[360,128]{1,0:T(8,128)S(1)}, f32[360,128]{1,0:T(8,128)S(1)}, u32[]{:S(2)}, u32[]{:S(2)}) collective-permute-start(f32[360,128]{1,0:T(8,128)S(1)} %get-tuple-element.61), channel_id=1, source_target_pairs={{0,1},{1,0},{2,3},{3,2},{4,5},{5,4},{6,7},{7,6},{8,9},{9,8},{10,11... | collective-permute-start | bytes 552968 | tf_op jit(solution)/shard_map/ppermute | solution.py:472
  31.9 9.0 %collective-permute-start.5 = (f32[360,128]{1,0:T(8,128)S(1)}, f32[360,128]{1,0:T(8,128)S(1)}, u32[]{:S(2)}, u32[]{:S(2)}) collective-permute-start(f32[360,128]{1,0:T(8,128)S(1)} %get-tuple-element.64), channel_id=1, source_target_pairs={{0,2},{1,0},{2,4},{3,1},{4,6},{5,3},{6,8},{7,5},{8,10},{9,7},{10,1... | collective-permute-start | bytes 552968 | tf_op jit(solution)/shard_map/ppermute | solution.py:465
  34.6 6.3 %collective-permute-start.6 = (f32[360,128]{1,0:T(8,128)S(1)}, f32[360,128]{1,0:T(8,128)S(1)}, u32[]{:S(2)}, u32[]{:S(2)}) collective-permute-start(f32[360,128]{1,0:T(8,128)S(1)} %get-tuple-element.63), channel_id=1, source_target_pairs={{0,4},{1,0},{2,6},{3,2},{4,8},{5,1},{6,10},{7,3},{8,12},{9,5},{10,... | collective-permute-start | bytes 552968 | tf_op jit(solution)/shard_map/ppermute | solution.py:466
  40.9 5.1 %collective-permute-start.7 = (f32[360,128]{1,0:T(8,128)S(1)}, f32[360,128]{1,0:T(8,128)S(1)}, u32[]{:S(2)}, u32[]{:S(2)}) collective-permute-start(f32[360,128]{1,0:T(8,128)S(1)} %select_select_fusion), channel_id=1, source_target_pairs={{0,1},{1,0},{2,3},{3,2},{4,5},{5,4},{6,7},{7,6},{8,9},{9,8},{10,11... | collective-permute-start | bytes 552968 | tf_op jit(solution)/shard_map/ppermute | solution.py:472
